TPU v7x, 256 devices: a whole 4x4x8 slice. The times are simulated.
256 devices in a mesh: head: 8 (over x, core), expert: 32 (over z, y).
Axes of the slice: x: 4, y: 4, z: 8, core: 2. Of those that a mesh axis runs over, the one named last changes fastest.
Arguments:
- queries: bfloat16 [512, 128, 576], P('expert', 'head'), may hold values from -64 to 64
- resident_cache: bfloat16 [128, 256, 576], P('expert'), may hold values from -6 to 6
- resident_len: int32 [128], P('expert'), may hold values from 1 to 256, as said below
- new_cache: bfloat16 [384, 64, 576], P('expert'), may hold values from -6 to 6
- new_len: int32 [384], replicated, may hold values from 1 to 64, as said below
- new_owner: int32 [384], replicated, may hold values from 0 to 31, as said below
- value_up: bfloat16 [128, 512, 128], P('head'), may hold values from -0.25 to 0.25
- w_output: bfloat16 [16384, 7168], P('head', 'expert'), may hold values from -0.046875 to 0.046875
- residual: bfloat16 [512, 7168], P(None, 'expert'), may hold values from -6 to 6
- expert_ids: int32 [512, 8], replicated, may hold values from 0 to 31, all different within a row; in each aligned block of 16 rows (0 to 15, 16 to 31, ...) at most 6 rows name the same one
- expert_gates: float32 [512, 8], replicated, may hold values from 0.1 to 1
- norm_gain: bfloat16 [7168], replicated, may hold values from 0.5 to 1.5
- w_gate: bfloat16 [32, 7168, 1024], P('expert', None, 'head'), may hold values from -0.0625 to 0.0625
- w_up: bfloat16 [32, 7168, 1024], P('expert', None, 'head'), may hold values from -0.0625 to 0.0625
- w_down: bfloat16 [32, 1024, 7168], P('expert', 'head'), may hold values from -0.1875 to 0.1875
Outputs:
- layer_out: bfloat16 [512, 7168], P('head', 'expert')
Inputs may be any that keep to these rules, and one draw needn't show every extreme that they name: `resident_len`: every decode owner has a resident request of length 256. `new_len`: every prefill device holds a new request of length 64. `new_owner`: one prefill device sends at most 2 of its 12 new requests to one decode owner, and every decode owner receives exactly 12 in all; a prefill device sends either 2 or none to each owner, except to at most one owner, which gets the remainder of 12 divided by 2. `expert_ids`: in each aligned block of 16 rows (the rows of one decode owner) no expert is named by more than 6 rows; the 8 experts of a row differ.
All inputs are finite; a program needn't handle non-finite values.
Results may differ from a plain program's by a relative error of at most 0.012.
Values may be sent and summed in bfloat16 or wider, within the bound.
No kernel may reach another device: no remote copies, remote signals or barrier semaphores. Data moves between devices by JAX's collectives and lax.ppermute only.
A program may use at most 128 MiB of HBM per device.

v0:
```python
import functools

import jax
import jax.numpy as jnp
from jax import lax
from jax.experimental import pallas as pl
from jax.experimental.pallas import tpu as pltpu
from jax.sharding import Mesh
from jax.sharding import PartitionSpec as P

ROPE = 64
NOPE = 128
EXPERT = ("expert_0", "expert_1", "expert_2")
COLUMN = EXPERT[1:]
HEAD = ("head_0", "head_1")
MOST = 2
CAP = 6
BF = jnp.bfloat16
F32 = jnp.float32
I32 = jnp.int32
VMEM_BYTES = 24 * 1024 * 1024


def params():
    return pltpu.CompilerParams(vmem_limit_bytes=VMEM_BYTES)


def whole(memory=pltpu.VMEM):
    return pl.BlockSpec(memory_space=memory)


def shifted(x, axis, step):
    n = lax.axis_size(axis)
    return lax.ppermute(x, axis, [(i, (i + step) % n) for i in range(n)])


def across(x, axis, mask):
    return lax.ppermute(x, axis, [(i, i ^ mask) for i in range(lax.axis_size(axis))])


def ring_gather(x, axis, dim):
    n = lax.axis_size(axis)
    far = n // 2
    cut = x.shape[dim] // 2
    found = {0: x}
    right, left = x, x
    for step in range(1, far):
        right, left = shifted(right, axis, 1), shifted(left, axis, -1)
        found[step], found[n - step] = right, left
    low = lax.slice_in_dim(right, 0, cut, axis=dim)
    high = lax.slice_in_dim(left, cut, x.shape[dim], axis=dim)
    found[far] = (shifted(low, axis, 1), shifted(high, axis, -1))
    return [found[d] for d in range(n)]


def flat(pieces):
    out = []
    for piece in pieces:
        out.extend(piece if isinstance(piece, tuple) else (piece,))
    return out


def attend(queries, caches_t, length, value_up):
    inverse_root = (NOPE + ROPE) ** (-0.5)
    latent_width = value_up.shape[1]
    scores = jnp.einsum("rhc,rct->rht", queries, caches_t, preferred_element_type=F32) * inverse_root
    inside = lax.broadcasted_iota(I32, scores.shape, 2) < length[:, None, None]
    scores = jnp.where(inside, scores, -jnp.inf)
    highest = jnp.max(scores, axis=2, keepdims=True)
    raised = jnp.exp(scores - highest)
    weights = (raised / jnp.sum(raised, axis=2, keepdims=True)).astype(BF)
    latent = jnp.einsum("rht,rct->rhc", weights, caches_t[:, :latent_width], preferred_element_type=F32).astype(BF)
    return jnp.einsum("rhc,hcv->hrv", latent, value_up, preferred_element_type=F32).astype(BF)


def pack_kernel(owners, cache_ref, out_ref, sems):
    count, span = cache_ref.shape[0], out_ref.shape[1]
    place, core = lax.axis_index(HEAD[0]), lax.axis_index(HEAD[1])
    base = lax.axis_index(EXPERT) * count
    first = pl.multiple_of(place * span, span)
    owner = [owners[base + i] for i in range(count)]
    turn = []
    for i in range(count):
        earlier = jnp.int32(0)
        for j in range(i):
            earlier = earlier + (owner[j] == owner[i]).astype(I32)
        turn.append(earlier)

    def copy(i):
        return pltpu.make_async_copy(
            cache_ref.at[i, pl.ds(first, span)], out_ref.at[owner[i]], sems.at[i]
        )

    for i in range(count):

        @pl.when(turn[i] == core)
        def _():
            copy(i).start()

    for i in range(count):

        @pl.when(turn[i] == core)
        def _():
            copy(i).wait()


def pack_cache(owners, cache, span, n_expert):
    return pl.pallas_call(
        pack_kernel,
        out_shape=jax.ShapeDtypeStruct((n_expert, span, cache.shape[2]), cache.dtype),
        in_specs=[whole(pltpu.SMEM), whole(pl.ANY)],
        out_specs=whole(pl.ANY),
        scratch_shapes=[pltpu.SemaphoreType.DMA((cache.shape[0],))],
        compiler_params=params(),
        name="pack_cache",
    )(owners, cache)


def select_kernel(sources, arrived_ref, out_ref, sems):
    copies = [
        pltpu.make_async_copy(arrived_ref.at[sources[k]], out_ref.at[k], sems.at[k])
        for k in range(out_ref.shape[0])
    ]
    for copy in copies:
        copy.start()
    for copy in copies:
        copy.wait()


def select_arrived(sources, arrived):
    count = sources.shape[0]
    return pl.pallas_call(
        select_kernel,
        out_shape=jax.ShapeDtypeStruct((count,) + arrived.shape[1:], arrived.dtype),
        in_specs=[whole(pltpu.SMEM), whole(pl.ANY)],
        out_specs=whole(pl.ANY),
        scratch_shapes=[pltpu.SemaphoreType.DMA((count,))],
        compiler_params=params(),
        name="select_arrived",
    )(sources, arrived)


def new_attention_kernel(groups, lens, at, q_ref, up_ref, res_ref, *refs):
    pieces, out_refs, latents = refs[: -groups - 1], refs[-groups - 1 : -1], refs[-1]
    ring = len(pieces) // 2
    pairs, span = pieces[0].shape[0], pieces[0].shape[1]
    old = res_ref.shape[1]
    count = pairs * MOST
    heads, latent_width, value_width = up_ref.shape
    inverse_root = (NOPE + ROPE) ** (-0.5)
    place, core, row = at[0], at[1], at[2]
    column = lax.broadcasted_iota(I32, (heads, ring * span), 1)
    position = ((place + ring - column // span) % ring) * span + column % span
    for i in range(count):
        k, turn = i // MOST, i % MOST
        ours = core == turn
        cache = jnp.concatenate(
            [jnp.where(ours, pieces[d][k], pieces[ring + d][k]) for d in range(ring)], axis=0
        )
        scores = (
            lax.dot_general(q_ref[old + i], cache, (((1,), (1,)), ((), ())), preferred_element_type=F32)
            * inverse_root
        )
        scores = jnp.where(position < lens[i], scores, -jnp.inf)
        raised = jnp.exp(scores - jnp.max(scores, axis=1, keepdims=True))
        weights = (raised / jnp.sum(raised, axis=1, keepdims=True)).astype(BF)
        latents[:, i, :] = jnp.dot(weights, cache[:, :latent_width], preferred_element_type=F32)
    each = heads // groups
    for d, out_ref in enumerate(out_refs):
        for k in range(each):
            h = lax.rem(row + d, groups) * each + k
            values = jnp.dot(latents[h].astype(BF), up_ref[h], preferred_element_type=F32)
            rows = jnp.concatenate([res_ref[h].astype(F32), values[:count]], axis=0).astype(BF)
            out_ref[:, k * value_width : (k + 1) * value_width] = rows


def new_attention(lens, at, queries, value_up, resident, pieces, groups):
    heads, latent_width, value_width = value_up.shape
    rows = queries.shape[0]
    out = jax.ShapeDtypeStruct((rows, heads // groups * value_width), BF)
    return pl.pallas_call(
        functools.partial(new_attention_kernel, groups),
        out_shape=(out,) * groups,
        in_specs=[whole(pltpu.SMEM)] * 2 + [whole()] * (3 + len(pieces)),
        out_specs=(whole(),) * groups,
        scratch_shapes=[pltpu.VMEM((heads, rows, latent_width), F32)],
        compiler_params=params(),
        name="new_attention",
    )(lens, at, queries, value_up, resident, *pieces)


def stack_kernel(*refs):
    rows = refs[0].shape[0]
    for k, ref in enumerate(refs[:-1]):
        refs[-1][k * rows : (k + 1) * rows, :] = ref[...]


def stacked(pieces):
    rows, width = pieces[0].shape
    return pl.pallas_call(
        stack_kernel,
        out_shape=jax.ShapeDtypeStruct((rows * len(pieces), width), pieces[0].dtype),
        in_specs=[whole()] * len(pieces),
        out_specs=whole(),
        compiler_params=params(),
        name="stack",
    )(*pieces)


def project_kernel(count, places, *refs):
    pieces, weights, out_ref = refs[:count], refs[count:-1], refs[-1]
    rows = out_ref.shape[2]
    attention = jnp.concatenate([piece[...] for piece in pieces], axis=0)
    for q, w in enumerate(weights):
        mixed = lax.dot_general(attention, w[...], (((1,), (1,)), ((), ())), preferred_element_type=F32).astype(BF)
        for k in range(attention.shape[0] // rows):
            out_ref[places[q, k], places[2, k]] = mixed[k * rows : (k + 1) * rows]


def project(places, pieces, weights, shape):
    return pl.pallas_call(
        functools.partial(project_kernel, len(pieces)),
        out_shape=jax.ShapeDtypeStruct(shape, BF),
        in_specs=[whole(pltpu.SMEM)] + [whole()] * (len(pieces) + len(weights)),
        out_specs=whole(),
        compiler_params=params(),
        name="project",
    )(places, *pieces, *weights)


def pair_kernel(a_ref, b_ref, *outs):
    for d, out in enumerate(outs):
        out[...] = (a_ref[d].astype(F32) + b_ref[d].astype(F32)).astype(out.dtype)


def pair_sum(a, b):
    out = jax.ShapeDtypeStruct(a.shape[1:], BF)
    return pl.pallas_call(
        pair_kernel,
        out_shape=(out,) * a.shape[0],
        in_specs=[whole()] * 2,
        out_specs=(whole(),) * a.shape[0],
        compiler_params=params(),
        name="pair_sum",
    )(a, b)


def plan_kernel(rows_dev, ids_ref, gates_ref, sel_ref, mix_ref):
    rows, choose = ids_ref.shape
    slots_all = sel_ref.shape[1]
    slots = rows // rows_dev * CAP
    experts = slots_all // slots
    expert = lax.broadcasted_iota(I32, (rows, experts), 1)
    member = jnp.zeros((rows, experts), F32)
    gate = jnp.zeros((rows, experts), F32)
    for k in range(choose):
        same = ids_ref[:, k : k + 1] == expert
        member = jnp.where(same, 1.0, member)
        gate = jnp.where(same, gates_ref[:, k : k + 1], gate)
    to_row = lax.broadcasted_iota(I32, (rows, rows), 0)
    from_row = lax.broadcasted_iota(I32, (rows, rows), 1)
    before = (from_row < to_row) & (from_row // rows_dev == to_row // rows_dev)
    rank = jnp.dot(before.astype(F32).astype(BF), member.astype(BF), preferred_element_type=F32)
    block = lax.broadcasted_iota(I32, (rows, experts), 0) // rows_dev
    slot = jnp.where(member > 0, rank + (block * CAP).astype(F32), -1.0)
    spread = (
        lax.broadcasted_iota(I32, (experts, slots_all), 0)
        == lax.broadcasted_iota(I32, (experts, slots_all), 1) // slots
    ).astype(F32)
    slot_wide = jnp.dot(slot.astype(BF), spread.astype(BF), preferred_element_type=F32)
    gate_wide = jnp.dot(gate, spread, preferred_element_type=F32, precision=lax.Precision.HIGHEST)
    wanted = (lax.broadcasted_iota(I32, (rows, slots_all), 1) % slots).astype(F32)
    hit = slot_wide == wanted
    sel_ref[...] = jnp.where(hit, 1.0, 0.0).astype(BF)
    mix_ref[...] = jnp.where(hit, gate_wide, 0.0)


def plan(ids, gates, rows_dev, experts):
    rows = ids.shape[0]
    slots_all = experts * (rows // rows_dev) * CAP
    return pl.pallas_call(
        functools.partial(plan_kernel, rows_dev),
        out_shape=(
            jax.ShapeDtypeStruct((rows, slots_all), BF),
            jax.ShapeDtypeStruct((rows, slots_all), F32),
        ),
        in_specs=[whole()] * 2,
        out_specs=(whole(), whole()),
        compiler_params=params(),
        name="plan",
    )(ids, gates)


def dispatch_kernel(parts_ref, residual_ref, sel_ref, hidden_ref, out_ref):
    total = parts_ref[0].astype(F32)
    for k in range(1, parts_ref.shape[0]):
        total = total + parts_ref[k].astype(F32)
    hidden = (residual_ref[...].astype(F32) + total).astype(BF)
    hidden_ref[...] = hidden
    picked = lax.dot_general(sel_ref[...], hidden, (((0,), (0,)), ((), ())), preferred_element_type=F32)
    out_ref[...] = picked.reshape(out_ref.shape).astype(BF)


def dispatch(parts, residual, sel, experts):
    rows, columns = residual.shape
    return pl.pallas_call(
        dispatch_kernel,
        out_shape=(
            jax.ShapeDtypeStruct((rows, columns), BF),
            jax.ShapeDtypeStruct((experts, sel.shape[1] // experts, columns), BF),
        ),
        in_specs=[whole()] * 3,
        out_specs=(whole(), whole()),
        compiler_params=params(),
        name="dispatch",
    )(parts, residual, sel)


def norm_kernel(x_ref, gain_ref, out_ref):
    count = x_ref.shape[0]
    squares = 0.0
    for j in range(count):
        x = x_ref[j].astype(F32)
        squares = squares + x * x
    mean = jnp.sum(squares, axis=1, keepdims=True) / out_ref.shape[1]
    inverse = lax.rsqrt(mean + 1e-06)
    x = jnp.concatenate([x_ref[j].astype(F32) for j in range(count)], axis=1)
    out_ref[...] = (x * inverse * gain_ref[...].astype(F32)).astype(BF)


def normed_rows(x, gain):
    return pl.pallas_call(
        norm_kernel,
        out_shape=jax.ShapeDtypeStruct((x.shape[1], x.shape[0] * x.shape[2]), BF),
        in_specs=[whole()] * 2,
        out_specs=whole(),
        compiler_params=params(),
        name="norm",
    )(x, gain)


def units_kernel(layout, *refs):
    count = sum(layout)
    x_refs, (gate_ref, up_ref, act_ref) = refs[:count], refs[count:]
    blocks, at = [], 0
    for parts in layout:
        blocks.append(jnp.concatenate([x_refs[at + p][...] for p in range(parts)], axis=1))
        at += parts
    x = jnp.concatenate(blocks, axis=0)
    gate = jnp.dot(x, gate_ref[...], preferred_element_type=F32)
    up = jnp.dot(x, up_ref[...], preferred_element_type=F32)
    act_ref[...] = (gate * jax.nn.sigmoid(gate) * up).astype(BF)


def run_units(layout, pieces, w_gate, w_up):
    slots = pieces[0].shape[0] * len(layout)
    return pl.pallas_call(
        functools.partial(units_kernel, layout),
        out_shape=jax.ShapeDtypeStruct((slots, w_gate.shape[1]), BF),
        in_specs=[whole()] * (len(pieces) + 2),
        out_specs=whole(),
        compiler_params=params(),
        name="units",
    )(*pieces, w_gate, w_up)


def down_kernel(*refs):
    ring = len(refs) // 2 - 1
    acts, downs, outs = refs[:ring], refs[ring : 2 * ring], refs[2 * ring :]
    slots = acts[0].shape[0] // (2 * ring)
    turned = []
    for d in range(ring):
        act = acts[d][...].astype(F32)
        order = [core * ring + (t + ring - d) % ring for core in range(2) for t in range(ring)]
        turned.append(jnp.concatenate([act[k * slots : (k + 1) * slots] for k in order], axis=0).astype(BF))
    units = jnp.concatenate(turned, axis=1)
    down = jnp.concatenate([w[...] for w in downs], axis=0)
    y = jnp.dot(units, down, preferred_element_type=F32).astype(BF)
    half = ring * slots
    for k, out in enumerate(outs):
        for t in range(ring):
            at = k * half + t * slots
            out[t] = y[at : at + slots]


def run_down(acts, downs):
    ring = len(acts)
    out = jax.ShapeDtypeStruct((ring, acts[0].shape[0] // (2 * ring), downs[0].shape[1]), BF)
    return pl.pallas_call(
        down_kernel,
        out_shape=(out, out),
        in_specs=[whole()] * (2 * ring),
        out_specs=(whole(), whole()),
        compiler_params=params(),
        name="down",
    )(*acts, *downs)


def columns_kernel(at, *refs):
    pieces, out_ref = refs[:-1], refs[-1]
    ring = len(pieces)
    each, width = out_ref.shape[0] // ring, out_ref.shape[2]
    for t, piece in enumerate(pieces):
        first = lax.rem(at[0] + t, ring) * each
        values = piece[...].astype(F32)
        for j in range(each):
            out_ref[first + j] = values[:, j * width : (j + 1) * width].astype(BF)


def by_columns(at, pieces, parts):
    slots, width = pieces[0].shape
    return pl.pallas_call(
        columns_kernel,
        out_shape=jax.ShapeDtypeStruct((parts, slots, width * len(pieces) // parts), BF),
        in_specs=[whole(pltpu.SMEM)] + [whole()] * len(pieces),
        out_specs=whole(),
        compiler_params=params(),
        name="by_columns",
    )(at, *pieces)


def combine_kernel(back_ref, mix_ref, hidden_ref, out_ref):
    back = back_ref[...].astype(F32).reshape(-1, back_ref.shape[2])
    routed = jnp.dot(mix_ref[...], back, preferred_element_type=F32, precision=lax.Precision.HIGHEST)
    out_ref[...] = (hidden_ref[...].astype(F32) + routed).astype(BF)


def combine(back, mix, hidden):
    return pl.pallas_call(
        combine_kernel,
        out_shape=jax.ShapeDtypeStruct(hidden.shape, BF),
        in_specs=[whole()] * 3,
        out_specs=whole(),
        compiler_params=params(),
        name="combine",
    )(back, mix, hidden)


def exchange(x, axes):
    return lax.all_to_all(x, axes, split_axis=0, concat_axis=0, tiled=True)


def gather_over_head(x):
    near = ring_gather(x, HEAD[0], 1)
    layout = [len(p) if isinstance(p, tuple) else 1 for p in near]
    near = flat(near)
    far = [shifted(p, HEAD[1], 1) for p in near]
    return tuple(layout * 2), near + far


def per_device(
    queries,
    resident_cache,
    resident_len,
    new_cache,
    new_len,
    new_owner,
    value_up,
    w_output,
    residual,
    expert_ids,
    expert_gates,
    norm_gain,
    w_gate,
    w_up,
    w_down,
):
    n_expert = lax.axis_size(EXPERT)
    n_head = lax.axis_size(HEAD)
    n_z, n_y = lax.axis_size(EXPERT[0]), lax.axis_size(COLUMN)
    z, y = lax.axis_index(EXPERT[0]), lax.axis_index(COLUMN)
    me = lax.axis_index(EXPERT)
    head = lax.axis_index(HEAD)
    req_count = resident_cache.shape[0]
    new_count = new_cache.shape[0]
    rows_dev = req_count + new_count
    rows_all = rows_dev * n_expert
    block_rows = rows_all // n_head
    columns = residual.shape[1]
    news = new_owner.shape[0]

    x, core = lax.axis_index(HEAD[0]), lax.axis_index(HEAD[1])
    ring = lax.axis_size(HEAD[0])
    number = jnp.arange(news, dtype=I32)
    equal = (new_owner[:, None] == new_owner[None, :]) & (number[None, :] < number[:, None])
    place = jnp.sum(equal.astype(I32), axis=1)
    mine = jnp.arange(new_count, dtype=I32)
    taken = (new_owner == me)[None, :] & (place[None, :] == mine[:, None])
    sources = jnp.sum(jnp.where(taken, (number // new_count)[None, :], 0), axis=1)[::MOST]
    lens = jnp.sum(jnp.where(taken, new_len[None, :], 0), axis=1)
    at = jnp.stack([x, core, y % 2]).astype(I32)

    packed = pack_cache(new_owner, new_cache, new_cache.shape[1] // ring, n_expert)
    resident = attend(queries[:req_count], jnp.swapaxes(resident_cache, 1, 2), resident_len, value_up)
    arrived, resident = lax.optimization_barrier((exchange(packed, EXPERT), resident))
    ours = select_arrived(sources, arrived)
    near = [ours] + [shifted(ours, HEAD[0], d) for d in range(1, ring)]
    pieces = near + [shifted(p, HEAD[1], 1) for p in near]
    attention = new_attention(lens, at, queries, value_up, resident, pieces, 2)

    w_t = w_output.T
    width = w_t.shape[1] // 2
    group = lambda d: lax.dynamic_slice_in_dim(w_t, ((y + d) % 2) * width, width, 1)
    weights = [group(0), across(group(1), COLUMN, 1)]
    along_y = list(attention[:1]) + [across(attention[d % 2], COLUMN, d) for d in range(1, n_y)]
    rows_here = flat(ring_gather(stacked(along_y), EXPERT[0], 0))
    w_d = w_down.reshape(w_down.shape[1:])
    part = w_d.shape[1] // ring
    some = lambda d: lax.dynamic_slice_in_dim(w_d, ((x + d) % ring) * part, part, 1)
    downs = [some(0)] + [shifted(some(d), HEAD[0], d) for d in range(1, ring)]
    downs, rows_here = lax.optimization_barrier((downs, rows_here))
    away = jnp.arange(n_expert, dtype=I32)
    maker_z = (z + n_z - away // n_y) % n_z
    maker_y = y ^ (away % n_y)
    per_head = n_expert // n_head
    maker_head = (maker_z * n_y + maker_y) // per_head
    places = jnp.stack([maker_head * 2 + y % 2, maker_head * 2 + (y + 1) % 2, (maker_z * n_y + maker_y) % per_head])
    mixed = project(places, rows_here, weights, (2 * n_head, per_head, rows_dev, columns))
    parts = exchange(mixed.reshape(2 * n_head, block_rows, columns), HEAD + COLUMN[1:])

    block = lambda a: lax.dynamic_slice_in_dim(a, head * block_rows, block_rows)
    sel, mix = plan(block(expert_ids), block(expert_gates), rows_dev, n_expert)
    hidden, outgoing = dispatch(parts, block(residual), sel, n_expert)
    received = exchange(outgoing, EXPERT)
    normed = normed_rows(received, norm_gain.reshape(1, -1))
    layout, pieces = gather_over_head(normed)
    act = run_units(layout, pieces, w_gate.reshape(w_gate.shape[1:]), w_up.reshape(w_up.shape[1:]))
    acts = [act] + [shifted(act, HEAD[0], d) for d in range(1, ring)]
    kept, sent = run_down(acts, downs)
    made = pair_sum(kept, shifted(sent, HEAD[1], 1))
    made = list(made[:1]) + [shifted(made[t], HEAD[0], -t) for t in range(1, ring)]
    back = exchange(by_columns(at, made, n_expert), EXPERT)
    return combine(back, mix, hidden)


def solution(mesh):
    finer = Mesh(mesh.devices.reshape(4, 2, 8, 2, 2), HEAD + EXPERT)
    in_specs = (
        P(EXPERT, HEAD, None),
        P(EXPERT, None, None),
        P(EXPERT),
        P(EXPERT, None, None),
        P(),
        P(),
        P(HEAD, None, None),
        P(HEAD, EXPERT),
        P(None, EXPERT),
        P(),
        P(),
        P(),
        P(EXPERT, None, HEAD),
        P(EXPERT, None, HEAD),
        P(EXPERT, HEAD, None),
    )
    out_specs = P(HEAD, EXPERT)
    return jax.shard_map(
        per_device, mesh=finer, in_specs=in_specs, out_specs=out_specs, check_vma=False
    )
```

profile of v0, /device:TPU:32, one launch (start us, length us, event | category | flops | bytes accessed | tf_op | source)
XLA Modules:
  0.0 198.5 jit_solution(16690385410699842682)
XLA Ops:
  3.3 11.5 %all-to-all-start = ((bf16[32,16,576]{2,1,0:T(8,128)(2,1)}), bf16[32,16,576]{2,1,0:T(8,128)(2,1)S(1)}, u32[]{:S(2)}, u32[]{:S(2)}) async-start(bf16[32,16,576]{2,1,0:T(8,128)(2,1)} %pack_cache.1), calls=%async_computation | async-start | bytes 1310720 | tf_op jit(solution)/shard_map/all_to_all | solution.py:440
  19.1 15.6 %all-to-all-done.arrived_ref = bf16[32,16,576]{2,1,0:T(8,128)(2,1)S(1)} async-done(((bf16[32,16,576]{2,1,0:T(8,128)(2,1)}), bf16[32,16,576]{2,1,0:T(8,128)(2,1)S(1)}, u32[]{:S(2)}, u32[]{:S(2)}) %all-to-all-start) | async-done | bytes 589856 | tf_op jit(solution)/shard_map/all_to_all | solution.py:440
  35.4 2.8 %collective-permute-start.5 = (bf16[6,16,576]{2,1,0:T(8,128)(2,1)S(1)}, bf16[6,16,576]{2,1,0:T(8,128)(2,1)S(1)}, u32[]{:S(2)}, u32[]{:S(2)}) collective-permute-start(bf16[6,16,576]{2,1,0:T(8,128)(2,1)S(1)} %select_arrived.1.refs_0_), channel_id=1, source_target_pairs={{0,192},{64,0},{128,64},{192,128},{1,193},{65,1},{129,65},{193,129... | collective-permute-start | bytes 331784 | tf_op jit(solution)/shard_map/ppermute | solution.py:34
  40.7 4.0 %collective-permute-done.4.refs_2_ = bf16[6,16,576]{2,1,0:T(8,128)(2,1)S(1)} collective-permute-done((bf16[6,16,576]{2,1,0:T(8,128)(2,1)S(1)}, bf16[6,16,576]{2,1,0:T(8,128)(2,1)S(1)}, u32[]{:S(2)}, u32[]{:S(2)}) %collective-permute-start.4) | collective-permute-done | bytes 110624 | tf_op jit(solution)/shard_map/ppermute | solution.py:34
  47.3 5.2 %new_attention.1 = (bf16[16,1024]{1,0:T(8,128)(2,1)S(1)}, bf16[16,1024]{1,0:T(8,128)(2,1)S(1)}) custom-call(s32[12]{0:T(128)S(1)} %get-tuple-element.60.lens, s32[3]{0:T(128)S(1)} %pad_add_fusion.1.at, bf16[16,16,576]{2,1,0:T(8,128)(2,1)S(1)} %copy-done.5, bf16[16,512,128]{2,1,0:T(8,128)(2,1)S(1)} %copy-done.1, ...), custom_call_target="tpu_custom_call" | custom-call | tf_op jit(solution)/shard_map/new_attention/pallas_call | solution.py:181
  61.7 2.9 %collective-permute-done.17.refs_8_ = bf16[64,1024]{1,0:T(8,128)(2,1)S(1)} collective-permute-done((bf16[64,1024]{1,0:T(8,128)(2,1)S(1)}, bf16[64,1024]{1,0:T(8,128)(2,1)S(1)}, u32[]{:S(2)}, u32[]{:S(2)}) %collective-permute-start.17) | collective-permute-done | bytes 131104 | tf_op jit(solution)/shard_map/ppermute | solution.py:34
  66.1 2.6 %dynamic-slice_bitcast_fusion.2 = (bf16[128,1792]{1,0:T(8,128)(2,1)}, bf16[128,1792]{1,0:T(8,128)(2,1)}, bf16[128,1792]{1,0:T(8,128)(2,1)S(1)}, bf16[128,1792]{1,0:T(8,128)(2,1)}) fusion(bf16[1,128,7168]{2,1,0:T(8,128)(2,1)} %param.29, s32[]{:T(128)S(6)} %select_n.175, s32[]{:T(128)S(6)} %select_n.171, s32[]{:T(128)S(6)} %select_n.169, s32[]{:T(128)S(6)} %select_n.173), kind=kLoop, calls=%fused_computation.13 | loop fusion | bytes 3670032 | tf_op jit(solution)/shard_map/dynamic_slice | solution.py:509
  79.4 3.4 %collective-permute-done.15.refs_3_ = bf16[64,1024]{1,0:T(8,128)(2,1)S(1)} collective-permute-done((bf16[64,1024]{1,0:T(8,128)(2,1)}, bf16[64,1024]{1,0:T(8,128)(2,1)S(1)}, u32[]{:S(2)}, u32[]{:S(2)}) %collective-permute-start.15) | collective-permute-done | bytes 131104 | tf_op jit(solution)/shard_map/ppermute | solution.py:34
  82.9 2.6 %collective-permute-start.20 = (bf16[32,1024]{1,0:T(8,128)(2,1)S(1)}, bf16[32,1024]{1,0:T(8,128)(2,1)S(1)}, u32[]{:S(2)}, u32[]{:S(2)}) collective-permute-start(bf16[32,1024]{1,0:T(8,128)(2,1)S(1)} %slice.30), channel_id=1, source_target_pairs={{0,28},{4,0},{8,4},{12,8},{16,12},{20,16},{24,20},{28,24},{1,29},{... | collective-permute-start | bytes 196616 | tf_op jit(solution)/shard_map/ppermute | solution.py:34
  85.6 4.3 %collective-permute-done.refs_5_ = bf16[128,1792]{1,0:T(8,128)(2,1)S(1)} collective-permute-done((bf16[128,1792]{1,0:T(8,128)(2,1)}, bf16[128,1792]{1,0:T(8,128)(2,1)S(1)}, u32[]{:S(2)}, u32[]{:S(2)}) %collective-permute-start) | collective-permute-done | bytes 458784 | tf_op jit(solution)/shard_map/ppermute | solution.py:34
  90.0 2.9 %project.1 = bf16[16,4,16,224]{3,2,1,0:T(8,128)(2,1)} custom-call(s32[3,32]{1,0:T(4,128)S(1)} %pad_add_fusion.places, bf16[64,1024]{1,0:T(8,128)(2,1)S(1)} %stack.24.refs_0_, bf16[64,1024]{1,0:T(8,128)(2,1)S(1)} %collective-permute-done.13.refs_1_, bf16[64,1024]{1,0:T(8,128)(2,1)} %collective-permute-done.14.refs_2_, ...), custom_call_target="tpu_custom_call" | custom-call | tf_op jit(solution)/shard_map/project/pallas_call | solution.py:221
  92.8 5.8 %all-to-all-start.1 = ((bf16[16,64,224]{2,1,0:T(8,128)(2,1)}), bf16[16,64,224]{2,1,0:T(8,128)(2,1)S(1)}, u32[]{:S(2)}, u32[]{:S(2)}) async-start(bf16[16,64,224]{2,1,0:T(8,128)(2,1)} %bitcast.10), calls=%async_computation.1 | async-start | bytes 1048576 | tf_op jit(solution)/shard_map/all_to_all | solution.py:440
  106.7 3.1 %all-to-all-done.1.parts_ref = bf16[16,64,224]{2,1,0:T(8,128)(2,1)S(1)} async-done(((bf16[16,64,224]{2,1,0:T(8,128)(2,1)}), bf16[16,64,224]{2,1,0:T(8,128)(2,1)S(1)}, u32[]{:S(2)}, u32[]{:S(2)}) %all-to-all-start.1) | async-done | bytes 458784 | tf_op jit(solution)/shard_map/all_to_all | solution.py:440
  112.4 8.5 %all-to-all-start.2 = ((bf16[32,24,224]{2,1,0:T(8,128)(2,1)}), bf16[32,24,224]{2,1,0:T(8,128)(2,1)S(1)}, u32[]{:S(2)}, u32[]{:S(2)}) async-start(bf16[32,24,224]{2,1,0:T(8,128)(2,1)} %copy-done.10), calls=%async_computation.2 | async-start | bytes 786432 | tf_op jit(solution)/shard_map/all_to_all | solution.py:440
  121.7 14.3 %all-to-all-done.2.x_ref = bf16[32,24,224]{2,1,0:T(8,128)(2,1)S(1)} async-done(((bf16[32,24,224]{2,1,0:T(8,128)(2,1)}), bf16[32,24,224]{2,1,0:T(8,128)(2,1)S(1)}, u32[]{:S(2)}, u32[]{:S(2)}) %all-to-all-start.2) | async-done | bytes 344096 | tf_op jit(solution)/shard_map/all_to_all | solution.py:440
  138.3 6.1 %collective-permute-done.24.refs_4_ = bf16[24,7168]{1,0:T(8,128)(2,1)S(1)} collective-permute-done((bf16[24,7168]{1,0:T(8,128)(2,1)S(1)}, bf16[24,7168]{1,0:T(8,128)(2,1)S(1)}, u32[]{:S(2)}, u32[]{:S(2)}) %collective-permute-start.24) | collective-permute-done | bytes 344096 | tf_op jit(solution)/shard_map/ppermute | solution.py:34
  144.4 2.1 %collective-permute-start.25 = (bf16[24,3584]{1,0:T(8,128)(2,1)S(1)}, bf16[24,3584]{1,0:T(8,128)(2,1)S(1)}, u32[]{:S(2)}, u32[]{:S(2)}) collective-permute-start(bf16[24,3584]{1,0:T(8,128)(2,1)S(1)} %slice.32), channel_id=1, source_target_pairs={{0,192},{64,0},{128,64},{192,128},{1,193},{65,1},{129,65},{193,129... | collective-permute-start | bytes 516104 | tf_op jit(solution)/shard_map/ppermute | solution.py:34
  147.2 2.7 %collective-permute-done.25.refs_3_ = bf16[24,3584]{1,0:T(8,128)(2,1)S(1)} collective-permute-done((bf16[24,3584]{1,0:T(8,128)(2,1)S(1)}, bf16[24,3584]{1,0:T(8,128)(2,1)S(1)}, u32[]{:S(2)}, u32[]{:S(2)}) %collective-permute-start.25) | collective-permute-done | bytes 172064 | tf_op jit(solution)/shard_map/ppermute | solution.py:34
  149.9 3.3 %collective-permute-done.23.refs_2_ = bf16[24,3584]{1,0:T(8,128)(2,1)S(1)} collective-permute-done((bf16[24,3584]{1,0:T(8,128)(2,1)S(1)}, bf16[24,3584]{1,0:T(8,128)(2,1)S(1)}, u32[]{:S(2)}, u32[]{:S(2)}) %collective-permute-start.23) | collective-permute-done | bytes 172064 | tf_op jit(solution)/shard_map/ppermute | solution.py:34
  159.9 2.3 %collective-permute-done.33.refs_3_ = bf16[192,128]{1,0:T(8,128)(2,1)S(1)} collective-permute-done((bf16[192,128]{1,0:T(8,128)(2,1)S(1)}, bf16[192,128]{1,0:T(8,128)(2,1)S(1)}, u32[]{:S(2)}, u32[]{:S(2)}) %collective-permute-start.33) | collective-permute-done | bytes 49184 | tf_op jit(solution)/shard_map/ppermute | solution.py:34
  167.0 2.1 %collective-permute-start.35 = (bf16[24,1792]{1,0:T(8,128)(2,1)S(1)}, bf16[24,1792]{1,0:T(8,128)(2,1)S(1)}, u32[]{:S(2)}, u32[]{:S(2)}) collective-permute-start(bf16[24,1792]{1,0:T(8,128)(2,1)S(1)} %get-tuple-element.54), channel_id=1, source_target_pairs={{0,192},{64,0},{128,64},{192,128},{1,193},{65,1},{129,65},{193,129... | collective-permute-start | bytes 258056 | tf_op jit(solution)/shard_map/ppermute | solution.py:34
  170.0 3.0 %collective-permute-done.35.refs_1_ = bf16[24,1792]{1,0:T(8,128)(2,1)S(1)} collective-permute-done((bf16[24,1792]{1,0:T(8,128)(2,1)S(1)}, bf16[24,1792]{1,0:T(8,128)(2,1)S(1)}, u32[]{:S(2)}, u32[]{:S(2)}) %collective-permute-start.35) | collective-permute-done | bytes 86048 | tf_op jit(solution)/shard_map/ppermute | solution.py:34
  173.0 2.8 %collective-permute-done.36.refs_2_ = bf16[24,1792]{1,0:T(8,128)(2,1)S(1)} collective-permute-done((bf16[24,1792]{1,0:T(8,128)(2,1)S(1)}, bf16[24,1792]{1,0:T(8,128)(2,1)S(1)}, u32[]{:S(2)}, u32[]{:S(2)}) %collective-permute-start.36) | collective-permute-done | bytes 86048 | tf_op jit(solution)/shard_map/ppermute | solution.py:34
  177.4 19.8 %all_to_all.20.back_ref = bf16[32,24,224]{2,1,0:T(8,128)(2,1)S(1)} all-to-all(bf16[32,24,224]{2,1,0:T(8,128)(2,1)S(1)} %by_columns.1), channel_id=1, replica_groups=mesh['head_0'=4,'head_1'=2,'expert_0'=8,'expert_1'=2,'expert_2'=2] {'exp..., dimensions={0} | all-to-all | bytes 688128 | tf_op jit(solution)/shard_map/all_to_all | solution.py:440
  (144 shorter events, 64.4 us)
Async XLA Ops:
  3.3 31.3 %all-to-all-start = ((bf16[32,16,576]{2,1,0:T(8,128)(2,1)}), bf16[32,16,576]{2,1,0:T(8,128)(2,1)S(1)}, u32[]{:S(2)}, u32[]{:S(2)}) async-start(bf16[32,16,576]{2,1,0:T(8,128)(2,1)} %pack_cache.1), calls=%async_computation | async-start | bytes 1310720 | tf_op jit(solution)/shard_map/all_to_all | solution.py:440
  38.3 6.5 %collective-permute-start.4 = (bf16[6,16,576]{2,1,0:T(8,128)(2,1)S(1)}, bf16[6,16,576]{2,1,0:T(8,128)(2,1)S(1)}, u32[]{:S(2)}, u32[]{:S(2)}) collective-permute-start(bf16[6,16,576]{2,1,0:T(8,128)(2,1)S(1)} %select_arrived.1.refs_0_), channel_id=1, source_target_pairs={{0,128},{64,192},{128,0},{192,64},{1,129},{65,193},{129,1},{193,65... | collective-permute-start | bytes 331784 | tf_op jit(solution)/shard_map/ppermute | solution.py:34
  39.1 6.9 %collective-permute-start.3 = (bf16[6,16,576]{2,1,0:T(8,128)(2,1)S(1)}, bf16[6,16,576]{2,1,0:T(8,128)(2,1)S(1)}, u32[]{:S(2)}, u32[]{:S(2)}) collective-permute-start(bf16[6,16,576]{2,1,0:T(8,128)(2,1)S(1)} %select_arrived.1.refs_0_), channel_id=1, source_target_pairs={{0,64},{64,128},{128,192},{192,0},{1,65},{65,129},{129,193},{193,1... | collective-permute-start | bytes 331784 | tf_op jit(solution)/shard_map/ppermute | solution.py:34
  39.9 6.1 %collective-permute-start.6 = (bf16[6,16,576]{2,1,0:T(8,128)(2,1)S(1)}, bf16[6,16,576]{2,1,0:T(8,128)(2,1)S(1)}, u32[]{:S(2)}, u32[]{:S(2)}) collective-permute-start(bf16[6,16,576]{2,1,0:T(8,128)(2,1)S(1)} %select_arrived.1.refs_0_), channel_id=1, source_target_pairs={{0,32},{32,0},{1,33},{33,1},{2,34},{34,2},{3,35},{35,3},{4,36},{36... | collective-permute-start | bytes 331784 | tf_op jit(solution)/shard_map/ppermute | solution.py:34
  61.2 10.4 %collective-permute-start.13 = (bf16[64,1024]{1,0:T(8,128)(2,1)S(1)}, bf16[64,1024]{1,0:T(8,128)(2,1)S(1)}, u32[]{:S(2)}, u32[]{:S(2)}) collective-permute-start(bf16[64,1024]{1,0:T(8,128)(2,1)S(1)} %stack.24.refs_0_), channel_id=1, source_target_pairs={{0,4},{4,8},{8,12},{12,16},{16,20},{20,24},{24,28},{28,0},{1,5},{5... | collective-permute-start | bytes 393224 | tf_op jit(solution)/shard_map/ppermute | solution.py:34
  64.7 7.4 %collective-permute-start.18 = (bf16[64,1024]{1,0:T(8,128)(2,1)S(1)}, bf16[64,1024]{1,0:T(8,128)(2,1)}, u32[]{:S(2)}, u32[]{:S(2)}) collective-permute-start(bf16[64,1024]{1,0:T(8,128)(2,1)S(1)} %collective-permute-done.17.refs_8_), channel_id=1, source_target_pairs={{0,28},{4,0},{8,4},{12,8},{16,12},{20,16},{24,20},{28,24},{1,29},{... | collective-permute-start | bytes 393224 | tf_op jit(solution)/shard_map/ppermute | solution.py:34
  68.7 16.8 %collective-permute-start.2 = (bf16[128,1792]{1,0:T(8,128)(2,1)}, bf16[128,1792]{1,0:T(8,128)(2,1)S(1)}, u32[]{:S(2)}, u32[]{:S(2)}) collective-permute-start(bf16[128,1792]{1,0:T(8,128)(2,1)} %get-tuple-element.61), channel_id=1, source_target_pairs={{0,192},{64,0},{128,64},{192,128},{1,193},{65,1},{129,65},{193,129... | collective-permute-start | bytes 1376264 | tf_op jit(solution)/shard_map/ppermute | solution.py:34
  69.3 20.7 %collective-permute-start = (bf16[128,1792]{1,0:T(8,128)(2,1)}, bf16[128,1792]{1,0:T(8,128)(2,1)S(1)}, u32[]{:S(2)}, u32[]{:S(2)}) collective-permute-start(bf16[128,1792]{1,0:T(8,128)(2,1)} %get-tuple-element.62), channel_id=1, source_target_pairs={{0,64},{64,128},{128,192},{192,0},{1,65},{65,129},{129,193},{193,1... | collective-permute-start | bytes 1376264 | tf_op jit(solution)/shard_map/ppermute | solution.py:34
  70.7 19.2 %collective-permute-start.1 = (bf16[128,1792]{1,0:T(8,128)(2,1)}, bf16[128,1792]{1,0:T(8,128)(2,1)S(1)}, u32[]{:S(2)}, u32[]{:S(2)}) collective-permute-start(bf16[128,1792]{1,0:T(8,128)(2,1)} %get-tuple-element.64), channel_id=1, source_target_pairs={{0,128},{64,192},{128,0},{192,64},{1,129},{65,193},{129,1},{193,65... | collective-permute-start | bytes 1376264 | tf_op jit(solution)/shard_map/ppermute | solution.py:34
  77.2 12.8 %collective-permute-start.21 = (bf16[224,1024]{1,0:T(8,128)(2,1)}, bf16[224,1024]{1,0:T(8,128)(2,1)S(1)}, u32[]{:S(2)}, u32[]{:S(2)}) collective-permute-start(bf16[224,1024]{1,0:T(8,128)(2,1)} %get-tuple-element.65), channel_id=1, source_target_pairs={{0,1},{1,0},{2,3},{3,2},{4,5},{5,4},{6,7},{7,6},{8,9},{9,8},{10,11... | collective-permute-start | bytes 1376264 | tf_op jit(solution)/shard_map/ppermute | solution.py:38
  82.9 7.1 %collective-permute-start.20 = (bf16[32,1024]{1,0:T(8,128)(2,1)S(1)}, bf16[32,1024]{1,0:T(8,128)(2,1)S(1)}, u32[]{:S(2)}, u32[]{:S(2)}) collective-permute-start(bf16[32,1024]{1,0:T(8,128)(2,1)S(1)} %slice.30), channel_id=1, source_target_pairs={{0,28},{4,0},{8,4},{12,8},{16,12},{20,16},{24,20},{28,24},{1,29},{... | collective-permute-start | bytes 196616 | tf_op jit(solution)/shard_map/ppermute | solution.py:34
  92.8 17.0 %all-to-all-start.1 = ((bf16[16,64,224]{2,1,0:T(8,128)(2,1)}), bf16[16,64,224]{2,1,0:T(8,128)(2,1)S(1)}, u32[]{:S(2)}, u32[]{:S(2)}) async-start(bf16[16,64,224]{2,1,0:T(8,128)(2,1)} %bitcast.10), calls=%async_computation.1 | async-start | bytes 1048576 | tf_op jit(solution)/shard_map/all_to_all | solution.py:440
  112.4 23.5 %all-to-all-start.2 = ((bf16[32,24,224]{2,1,0:T(8,128)(2,1)}), bf16[32,24,224]{2,1,0:T(8,128)(2,1)S(1)}, u32[]{:S(2)}, u32[]{:S(2)}) async-start(bf16[32,24,224]{2,1,0:T(8,128)(2,1)} %copy-done.10), calls=%async_computation.2 | async-start | bytes 786432 | tf_op jit(solution)/shard_map/all_to_all | solution.py:440
  136.2 8.2 %collective-permute-start.24 = (bf16[24,7168]{1,0:T(8,128)(2,1)S(1)}, bf16[24,7168]{1,0:T(8,128)(2,1)S(1)}, u32[]{:S(2)}, u32[]{:S(2)}) collective-permute-start(bf16[24,7168]{1,0:T(8,128)(2,1)S(1)} %norm.1.refs_0_), channel_id=1, source_target_pairs={{0,192},{64,0},{128,64},{192,128},{1,193},{65,1},{129,65},{193,129... | collective-permute-start | bytes 1032200 | tf_op jit(solution)/shard_map/ppermute | solution.py:34
  136.7 9.8 %collective-permute-start.22 = (bf16[24,7168]{1,0:T(8,128)(2,1)S(1)}, bf16[24,7168]{1,0:T(8,128)(2,1)S(1)}, u32[]{:S(2)}, u32[]{:S(2)}) collective-permute-start(bf16[24,7168]{1,0:T(8,128)(2,1)S(1)} %norm.1.refs_0_), channel_id=1, source_target_pairs={{0,64},{64,128},{128,192},{192,0},{1,65},{65,129},{129,193},{193,1... | collective-permute-start | bytes 1032200 | tf_op jit(solution)/shard_map/ppermute | solution.py:34
  138.3 15.0 %collective-permute-start.26 = (bf16[24,7168]{1,0:T(8,128)(2,1)S(1)}, bf16[24,7168]{1,0:T(8,128)(2,1)S(1)}, u32[]{:S(2)}, u32[]{:S(2)}) collective-permute-start(bf16[24,7168]{1,0:T(8,128)(2,1)S(1)} %norm.1.refs_0_), channel_id=1, source_target_pairs={{0,32},{32,0},{1,33},{33,1},{2,34},{34,2},{3,35},{35,3},{4,36},{36... | collective-permute-start | bytes 1032200 | tf_op jit(solution)/shard_map/ppermute | solution.py:34
  146.5 6.7 %collective-permute-start.23 = (bf16[24,3584]{1,0:T(8,128)(2,1)S(1)}, bf16[24,3584]{1,0:T(8,128)(2,1)S(1)}, u32[]{:S(2)}, u32[]{:S(2)}) collective-permute-start(bf16[24,3584]{1,0:T(8,128)(2,1)S(1)} %slice.31), channel_id=1, source_target_pairs={{0,64},{64,128},{128,192},{192,0},{1,65},{65,129},{129,193},{193,1... | collective-permute-start | bytes 516104 | tf_op jit(solution)/shard_map/ppermute | solution.py:34
  146.6 6.6 %collective-permute-start.30 = (bf16[24,7168]{1,0:T(8,128)(2,1)S(1)}, bf16[24,7168]{1,0:T(8,128)(2,1)S(1)}, u32[]{:S(2)}, u32[]{:S(2)}) collective-permute-start(bf16[24,7168]{1,0:T(8,128)(2,1)S(1)} %collective-permute-done.24.refs_4_), channel_id=1, source_target_pairs={{0,32},{32,0},{1,33},{33,1},{2,34},{34,2},{3,35},{35,3},{4,36},{36... | collective-permute-start | bytes 1032200 | tf_op jit(solution)/shard_map/ppermute | solution.py:34
  146.7 7.9 %collective-permute-start.27 = (bf16[24,7168]{1,0:T(8,128)(2,1)S(1)}, bf16[24,7168]{1,0:T(8,128)(2,1)S(1)}, u32[]{:S(2)}, u32[]{:S(2)}) collective-permute-start(bf16[24,7168]{1,0:T(8,128)(2,1)S(1)} %collective-permute-done.22.refs_1_), channel_id=1, source_target_pairs={{0,32},{32,0},{1,33},{33,1},{2,34},{34,2},{3,35},{35,3},{4,36},{36... | collective-permute-start | bytes 1032200 | tf_op jit(solution)/shard_map/ppermute | solution.py:34
  158.0 5.7 %collective-permute-start.32 = (bf16[192,128]{1,0:T(8,128)(2,1)S(1)}, bf16[192,128]{1,0:T(8,128)(2,1)S(1)}, u32[]{:S(2)}, u32[]{:S(2)}) collective-permute-start(bf16[192,128]{1,0:T(8,128)(2,1)S(1)} %units.1.refs_0_), channel_id=1, source_target_pairs={{0,128},{64,192},{128,0},{192,64},{1,129},{65,193},{129,1},{193,65... | collective-permute-start | bytes 147464 | tf_op jit(solution)/shard_map/ppermute | solution.py:34
  158.7 5.9 %collective-permute-start.31 = (bf16[192,128]{1,0:T(8,128)(2,1)S(1)}, bf16[192,128]{1,0:T(8,128)(2,1)S(1)}, u32[]{:S(2)}, u32[]{:S(2)}) collective-permute-start(bf16[192,128]{1,0:T(8,128)(2,1)S(1)} %units.1.refs_0_), channel_id=1, source_target_pairs={{0,64},{64,128},{128,192},{192,0},{1,65},{65,129},{129,193},{193,1... | collective-permute-start | bytes 147464 | tf_op jit(solution)/shard_map/ppermute | solution.py:34
  167.0 6.1 %collective-permute-start.35 = (bf16[24,1792]{1,0:T(8,128)(2,1)S(1)}, bf16[24,1792]{1,0:T(8,128)(2,1)S(1)}, u32[]{:S(2)}, u32[]{:S(2)}) collective-permute-start(bf16[24,1792]{1,0:T(8,128)(2,1)S(1)} %get-tuple-element.54), channel_id=1, source_target_pairs={{0,192},{64,0},{128,64},{192,128},{1,193},{65,1},{129,65},{193,129... | collective-permute-start | bytes 258056 | tf_op jit(solution)/shard_map/ppermute | solution.py:34
  169.1 6.7 %collective-permute-start.36 = (bf16[24,1792]{1,0:T(8,128)(2,1)S(1)}, bf16[24,1792]{1,0:T(8,128)(2,1)S(1)}, u32[]{:S(2)}, u32[]{:S(2)}) collective-permute-start(bf16[24,1792]{1,0:T(8,128)(2,1)S(1)} %get-tuple-element.55), channel_id=1, source_target_pairs={{0,128},{64,192},{128,0},{192,64},{1,129},{65,193},{129,1},{193,65... | collective-permute-start | bytes 258056 | tf_op jit(solution)/shard_map/ppermute | solution.py:34
  170.0 6.7 %collective-permute-start.37 = (bf16[24,1792]{1,0:T(8,128)(2,1)S(1)}, bf16[24,1792]{1,0:T(8,128)(2,1)S(1)}, u32[]{:S(2)}, u32[]{:S(2)}) collective-permute-start(bf16[24,1792]{1,0:T(8,128)(2,1)S(1)} %get-tuple-element.56), channel_id=1, source_target_pairs={{0,64},{64,128},{128,192},{192,0},{1,65},{65,129},{129,193},{193,1... | collective-permute-start | bytes 258056 | tf_op jit(solution)/shard_map/ppermute | solution.py:34
  (40 other events, 406.5 us)
where the time goes:
time: 199 us; the launch traced here: 198 us
  waiting for transfers between devices  82.8 us (42%)
  starting transfers between devices  57.2 us (29%)
  blocking collectives  19.8 us (10%)
  local copies, waits for them, and re-layouts  18.6 us (9%)
  Pallas kernels  15.4 us (8%)
  matrix products  3.56 us (2%)
    ppermute x34, waiting for transfers between devices, shifted(): return lax.ppermute(x, axis, [(i, (i + step) % n) for i in range(n)])  46.2 us
    all_to_all x3, waiting for transfers between devices, exchange(): return lax.all_to_all(x, axes, split_axis=0, concat_axis=0, tiled=True)  32.9 us
    ppermute x34, starting transfers between devices, shifted(): return lax.ppermute(x, axis, [(i, (i + step) % n) for i in range(n)])  27.9 us
    all_to_all x3, starting transfers between devices, exchange(): return lax.all_to_all(x, axes, split_axis=0, concat_axis=0, tiled=True)  25.7 us
    all_to_all x1, blocking collectives, exchange(): return lax.all_to_all(x, axes, split_axis=0, concat_axis=0, tiled=True)  19.8 us
    unnamed x49, local copies, waits for them, and re-layouts  10.8 us
    pallas_call x1, Pallas kernels, new_attention(): pl.pallas_call(functools.partial(new_attention_kernel, groups), out_shape...  5.17 us
  transfers between devices with their start and end apart: 41, of which 25 were waited for; matrix products, arithmetic and copies ran while one was open for 7% of the time, Pallas kernels for 0%

commit v1 on v0

--- a/solution.py
+++ b/solution.py
@@ -140,10 +140,9 @@
     )(sources, arrived)
 
 
-def new_attention_kernel(groups, lens, at, q_ref, up_ref, res_ref, *refs):
-    pieces, out_refs, latents = refs[: -groups - 1], refs[-groups - 1 : -1], refs[-1]
-    ring = len(pieces) // 2
-    pairs, span = pieces[0].shape[0], pieces[0].shape[1]
+def new_attention_kernel(groups, lens, at, q_ref, up_ref, res_ref, near_ref, far_ref, *refs):
+    out_refs, latents = refs[:-1], refs[-1]
+    ring, pairs, span = near_ref.shape[:3]
     old = res_ref.shape[1]
     count = pairs * MOST
     heads, latent_width, value_width = up_ref.shape
@@ -155,7 +154,7 @@
         k, turn = i // MOST, i % MOST
         ours = core == turn
         cache = jnp.concatenate(
-            [jnp.where(ours, pieces[d][k], pieces[ring + d][k]) for d in range(ring)], axis=0
+            [jnp.where(ours, near_ref[d, k], far_ref[d, k]) for d in range(ring)], axis=0
         )
         scores = (
             lax.dot_general(q_ref[old + i], cache, (((1,), (1,)), ((), ())), preferred_element_type=F32)
@@ -174,19 +173,19 @@
             out_ref[:, k * value_width : (k + 1) * value_width] = rows
 
 
-def new_attention(lens, at, queries, value_up, resident, pieces, groups):
+def new_attention(lens, at, queries, value_up, resident, near, far, groups):
     heads, latent_width, value_width = value_up.shape
     rows = queries.shape[0]
     out = jax.ShapeDtypeStruct((rows, heads // groups * value_width), BF)
     return pl.pallas_call(
         functools.partial(new_attention_kernel, groups),
         out_shape=(out,) * groups,
-        in_specs=[whole(pltpu.SMEM)] * 2 + [whole()] * (3 + len(pieces)),
+        in_specs=[whole(pltpu.SMEM)] * 2 + [whole()] * 5,
         out_specs=(whole(),) * groups,
         scratch_shapes=[pltpu.VMEM((heads, rows, latent_width), F32)],
         compiler_params=params(),
         name="new_attention",
-    )(lens, at, queries, value_up, resident, *pieces)
+    )(lens, at, queries, value_up, resident, near, far)
 
 
 def stack_kernel(*refs):
@@ -204,6 +203,22 @@
         out_specs=whole(),
         compiler_params=params(),
         name="stack",
+    )(*pieces)
+
+
+def layers_kernel(*refs):
+    for k, ref in enumerate(refs[:-1]):
+        refs[-1][k] = ref[...]
+
+
+def layers(pieces):
+    return pl.pallas_call(
+        layers_kernel,
+        out_shape=jax.ShapeDtypeStruct((len(pieces),) + pieces[0].shape, pieces[0].dtype),
+        in_specs=[whole()] * len(pieces),
+        out_specs=whole(),
+        compiler_params=params(),
+        name="layers",
     )(*pieces)
 
 
@@ -492,23 +507,26 @@
 
     packed = pack_cache(new_owner, new_cache, new_cache.shape[1] // ring, n_expert)
     resident = attend(queries[:req_count], jnp.swapaxes(resident_cache, 1, 2), resident_len, value_up)
-    arrived, resident = lax.optimization_barrier((exchange(packed, EXPERT), resident))
-    ours = select_arrived(sources, arrived)
-    near = [ours] + [shifted(ours, HEAD[0], d) for d in range(1, ring)]
-    pieces = near + [shifted(p, HEAD[1], 1) for p in near]
-    attention = new_attention(lens, at, queries, value_up, resident, pieces, 2)
-
-    w_t = w_output.T
-    width = w_t.shape[1] // 2
+
+    packed, w_t, w_d = lax.optimization_barrier((packed, w_output.T, w_down.reshape(w_down.shape[1:])))
+    width, part = w_t.shape[1] // 2, w_d.shape[1] // ring
     group = lambda d: lax.dynamic_slice_in_dim(w_t, ((y + d) % 2) * width, width, 1)
     weights = [group(0), across(group(1), COLUMN, 1)]
+    downs = [lax.dynamic_slice_in_dim(w_d, ((x + d) % ring) * part, part, 1) for d in range(ring)]
+    for d in (1, 3):
+        downs[d] = shifted(downs[d], HEAD[0], d)
+    arrived, resident, weights, downs = lax.optimization_barrier(
+        (exchange(packed, EXPERT), resident, weights, downs)
+    )
+    ours = select_arrived(sources, arrived)
+    near = layers([ours] + [shifted(ours, HEAD[0], d) for d in range(1, ring)])
+    attention = new_attention(lens, at, queries, value_up, resident, near, shifted(near, HEAD[1], 1), 2)
     along_y = list(attention[:1]) + [across(attention[d % 2], COLUMN, d) for d in range(1, n_y)]
     rows_here = flat(ring_gather(stacked(along_y), EXPERT[0], 0))
-    w_d = w_down.reshape(w_down.shape[1:])
-    part = w_d.shape[1] // ring
-    some = lambda d: lax.dynamic_slice_in_dim(w_d, ((x + d) % ring) * part, part, 1)
-    downs = [some(0)] + [shifted(some(d), HEAD[0], d) for d in range(1, ring)]
-    downs, rows_here = lax.optimization_barrier((downs, rows_here))
+    downs[2] = shifted(downs[2], HEAD[0], 2)
+    block = lambda a: lax.dynamic_slice_in_dim(a, head * block_rows, block_rows)
+    planned = plan(block(expert_ids), block(expert_gates), rows_dev, n_expert)
+    downs, rows_here, (sel, mix), kept = lax.optimization_barrier((downs, rows_here, planned, block(residual)))
     away = jnp.arange(n_expert, dtype=I32)
     maker_z = (z + n_z - away // n_y) % n_z
     maker_y = y ^ (away % n_y)
@@ -518,9 +536,7 @@
     mixed = project(places, rows_here, weights, (2 * n_head, per_head, rows_dev, columns))
     parts = exchange(mixed.reshape(2 * n_head, block_rows, columns), HEAD + COLUMN[1:])
 
-    block = lambda a: lax.dynamic_slice_in_dim(a, head * block_rows, block_rows)
-    sel, mix = plan(block(expert_ids), block(expert_gates), rows_dev, n_expert)
-    hidden, outgoing = dispatch(parts, block(residual), sel, n_expert)
+    hidden, outgoing = dispatch(parts, kept, sel, n_expert)
     received = exchange(outgoing, EXPERT)
     normed = normed_rows(received, norm_gain.reshape(1, -1))
     layout, pieces = gather_over_head(normed)

time: 199 us -> 196 us (0.985)
  blocking collectives: 19.8 us -> 33.8 us
  waiting for transfers between devices: 82.8 us -> 73.2 us
  local copies, waits for them, and re-layouts: 18.6 us -> 11.5 us
  starting transfers between devices: 57.2 us -> 54.5 us
    all_to_all x3 -> x2, waiting for transfers between devices: 32.9 us -> 15 us  [exchange(): return lax.all_to_all(x, axes, split_axis=0, concat_axis=0, tiled=True)]
    all_to_all x1 -> x2, blocking collectives: 19.8 us -> 33.8 us  [exchange(): return lax.all_to_all(x, axes, split_axis=0, concat_axis=0, tiled=True)]
    ppermute x4, waiting for transfers between devices: 3.59 us -> 10.7 us  [across(): lax.ppermute(x, axis, [(i, i ^ mask) for i in range(lax.axis_size(axis))])]
    unnamed x49 -> x34, local copies, waits for them, and re-layouts: 10.8 us -> 6.38 us
    all_to_all x3 -> x2, starting transfers between devices: 25.7 us -> 22 us  [exchange(): return lax.all_to_all(x, axes, split_axis=0, concat_axis=0, tiled=True)]
    ppermute x34 -> x31, waiting for transfers between devices: 46.2 us -> 47.5 us  [shifted(): return lax.ppermute(x, axis, [(i, (i + step) % n) for i in range(n)])]
    ppermute x34 -> x31, starting transfers between devices: 27.9 us -> 27.3 us  [shifted(): return lax.ppermute(x, axis, [(i, (i + step) % n) for i in range(n)])]
  transfers between devices with their start and end apart: 41 -> 37, of which waited for: 25 -> 28; matrix products, arithmetic and copies ran while one was open for 7% -> 6% of each run, Pallas kernels for 0% -> 0%
where the time goes in v1:
time: 196 us; the launch traced here: 195 us
  waiting for transfers between devices  73.2 us (37%)
  starting transfers between devices  54.5 us (28%)
  blocking collectives  33.8 us (17%)
  Pallas kernels  16 us (8%)
  local copies, waits for them, and re-layouts  11.5 us (6%)
  matrix products  5.08 us (3%)
    ppermute x31, waiting for transfers between devices, shifted(): return lax.ppermute(x, axis, [(i, (i + step) % n) for i in range(n)])  47.5 us
    all_to_all x2, blocking collectives, exchange(): return lax.all_to_all(x, axes, split_axis=0, concat_axis=0, tiled=True)  33.8 us
    ppermute x31, starting transfers between devices, shifted(): return lax.ppermute(x, axis, [(i, (i + step) % n) for i in range(n)])  27.3 us
    all_to_all x2, starting transfers between devices, exchange(): return lax.all_to_all(x, axes, split_axis=0, concat_axis=0, tiled=True)  22 us
    all_to_all x2, waiting for transfers between devices, exchange(): return lax.all_to_all(x, axes, split_axis=0, concat_axis=0, tiled=True)  15 us
    ppermute x4, waiting for transfers between devices, across(): lax.ppermute(x, axis, [(i, i ^ mask) for i in range(lax.axis_size(axis))])  10.7 us
    unnamed x34, local copies, waits for them, and re-layouts  6.38 us
    pallas_call x1, Pallas kernels, new_attention(): pl.pallas_call(functools.partial(new_attention_kernel, groups), out_shape...  5.66 us
  transfers between devices with their start and end apart: 37, of which 28 were waited for; matrix products, arithmetic and copies ran while one was open for 6% of the time, Pallas kernels for 0%

profile of v1, /device:TPU:32, one launch (start us, length us, event | category | flops | bytes accessed | tf_op | source)
XLA Modules:
  0.0 195.2 jit_solution(10938076535667303473)
XLA Ops:
  3.3 11.5 %all-to-all-start = ((bf16[32,16,576]{2,1,0:T(8,128)(2,1)}), bf16[32,16,576]{2,1,0:T(8,128)(2,1)S(1)}, u32[]{:S(2)}, u32[]{:S(2)}) async-start(bf16[32,16,576]{2,1,0:T(8,128)(2,1)} %pack_cache.1), calls=%async_computation | async-start | bytes 1310720 | tf_op jit(solution)/shard_map/all_to_all | solution.py:455
  14.8 2.2 %constant_dynamic-slice_fusion.7 = (bf16[224,1024]{1,0:T(8,128)(2,1)}, bf16[224,1024]{1,0:T(8,128)(2,1)}) fusion(bf16[224,2048]{1,0:T(8,128)(2,1)} %bitcast.19, s32[]{:T(128)S(6)} %select_n.170, s32[]{:T(128)S(6)} %select_n.169), kind=kLoop, calls=%fused_computation.30 | loop fusion | bytes 1835016 | tf_op jit(solution)/shard_map/dynamic_slice | solution.py:513
  19.6 2.8 %collective-permute-start.2 = (bf16[128,1792]{1,0:T(8,128)(2,1)}, bf16[128,1792]{1,0:T(8,128)(2,1)}, u32[]{:S(2)}, u32[]{:S(2)}) collective-permute-start(bf16[128,1792]{1,0:T(8,128)(2,1)} %get-tuple-element.85), channel_id=1, source_target_pairs={{0,192},{64,0},{128,64},{192,128},{1,193},{65,1},{129,65},{193,129... | collective-permute-start | bytes 1376264 | tf_op jit(solution)/shard_map/ppermute | solution.py:34
  24.7 2.3 %fusion.4 = bf16[4,16,512]{2,1,0:T(8,128)(2,1)} fusion(bf16[4,576,256]{2,1,0:T(8,128)(2,1)} %bitcast.18, f32[4,16]{1,0:T(4,128)S(1)} %fusion.19, f32[4,16,256]{2,1,0:T(8,128)S(1)} %fusion.2), kind=kOutput, calls=%fused_computation.6 | convolution fusion | flops 16826688 | bytes 1247232 | tf_op jit(solution)/shard_map/rht,rct->rhc/dot_general | solution.py:72
  28.2 6.2 %collective-permute-done.refs_10_ = bf16[224,1024]{1,0:T(8,128)(2,1)} collective-permute-done((bf16[224,1024]{1,0:T(8,128)(2,1)}, bf16[224,1024]{1,0:T(8,128)(2,1)}, u32[]{:S(2)}, u32[]{:S(2)}) %collective-permute-start) | collective-permute-done | bytes 458784 | tf_op jit(solution)/shard_map/ppermute | solution.py:38
  35.9 2.4 %collective-permute-start.6 = (bf16[6,16,576]{2,1,0:T(8,128)(2,1)S(1)}, bf16[6,16,576]{2,1,0:T(8,128)(2,1)S(1)}, u32[]{:S(2)}, u32[]{:S(2)}) collective-permute-start(bf16[6,16,576]{2,1,0:T(8,128)(2,1)S(1)} %select_arrived.1.refs_0_), channel_id=1, source_target_pairs={{0,192},{64,0},{128,64},{192,128},{1,193},{65,1},{129,65},{193,129... | collective-permute-start | bytes 331784 | tf_op jit(solution)/shard_map/ppermute | solution.py:34
  39.9 2.4 %collective-permute-done.6.refs_3_ = bf16[6,16,576]{2,1,0:T(8,128)(2,1)S(1)} collective-permute-done((bf16[6,16,576]{2,1,0:T(8,128)(2,1)S(1)}, bf16[6,16,576]{2,1,0:T(8,128)(2,1)S(1)}, u32[]{:S(2)}, u32[]{:S(2)}) %collective-permute-start.6) | collective-permute-done | bytes 110624 | tf_op jit(solution)/shard_map/ppermute | solution.py:34
  42.3 2.4 %collective-permute-done.5.refs_2_ = bf16[6,16,576]{2,1,0:T(8,128)(2,1)S(1)} collective-permute-done((bf16[6,16,576]{2,1,0:T(8,128)(2,1)S(1)}, bf16[6,16,576]{2,1,0:T(8,128)(2,1)S(1)}, u32[]{:S(2)}, u32[]{:S(2)}) %collective-permute-start.5) | collective-permute-done | bytes 110624 | tf_op jit(solution)/shard_map/ppermute | solution.py:34
  49.1 5.7 %new_attention.1 = (bf16[16,1024]{1,0:T(8,128)(2,1)S(1)}, bf16[16,1024]{1,0:T(8,128)(2,1)S(1)}) custom-call(s32[12]{0:T(128)S(1)} %get-tuple-element.84.lens, s32[3]{0:T(128)S(1)} %pad_add_fusion.1.at, bf16[16,16,576]{2,1,0:T(8,128)(2,1)S(1)} %copy-done.6, bf16[16,512,128]{2,1,0:T(8,128)(2,1)S(1)} %copy-done.1, ...), custom_call_target="tpu_custom_call" | custom-call | tf_op jit(solution)/shard_map/new_attention/pallas_call | solution.py:180
  54.7 3.1 %collective-permute-start.9 = (bf16[16,1024]{1,0:T(8,128)(2,1)S(1)}, bf16[16,1024]{1,0:T(8,128)(2,1)S(1)}, u32[]{:S(2)}, u32[]{:S(2)}) collective-permute-start(bf16[16,1024]{1,0:T(8,128)(2,1)S(1)} %get-tuple-element.53.refs_0_), channel_id=1, source_target_pairs={{0,2},{1,3},{2,0},{3,1},{4,6},{5,7},{6,4},{7,5},{8,10},{9,11},{10,... | collective-permute-start | bytes 98312 | tf_op jit(solution)/shard_map/ppermute | solution.py:38
  60.2 2.7 %collective-permute-done.10.refs_3_ = bf16[16,1024]{1,0:T(8,128)(2,1)S(1)} collective-permute-done((bf16[16,1024]{1,0:T(8,128)(2,1)S(1)}, bf16[16,1024]{1,0:T(8,128)(2,1)S(1)}, u32[]{:S(2)}, u32[]{:S(2)}) %collective-permute-start.10) | collective-permute-done | bytes 32800 | tf_op jit(solution)/shard_map/ppermute | solution.py:38
  73.0 2.3 %collective-permute-start.17 = (bf16[64,1024]{1,0:T(8,128)(2,1)S(1)}, bf16[64,1024]{1,0:T(8,128)(2,1)S(1)}, u32[]{:S(2)}, u32[]{:S(2)}) collective-permute-start(bf16[64,1024]{1,0:T(8,128)(2,1)S(1)} %collective-permute-done.16.refs_7_), channel_id=1, source_target_pairs={{0,28},{4,0},{8,4},{12,8},{16,12},{20,16},{24,20},{28,24},{1,29},{... | collective-permute-start | bytes 393224 | tf_op jit(solution)/shard_map/ppermute | solution.py:34
  78.7 3.4 %collective-permute-start.18 = (bf16[32,1024]{1,0:T(8,128)(2,1)S(1)}, bf16[32,1024]{1,0:T(8,128)(2,1)S(1)}, u32[]{:S(2)}, u32[]{:S(2)}) collective-permute-start(bf16[32,1024]{1,0:T(8,128)(2,1)S(1)} %slice.30), channel_id=1, source_target_pairs={{0,28},{4,0},{8,4},{12,8},{16,12},{20,16},{24,20},{28,24},{1,29},{... | collective-permute-start | bytes 196616 | tf_op jit(solution)/shard_map/ppermute | solution.py:34
  84.5 3.7 %collective-permute-done.14.refs_4_ = bf16[32,1024]{1,0:T(8,128)(2,1)S(1)} collective-permute-done((bf16[32,1024]{1,0:T(8,128)(2,1)S(1)}, bf16[32,1024]{1,0:T(8,128)(2,1)S(1)}, u32[]{:S(2)}, u32[]{:S(2)}) %collective-permute-start.14) | collective-permute-done | bytes 65568 | tf_op jit(solution)/shard_map/ppermute | solution.py:34
  91.0 14.0 %all_to_all.20.parts_ref = bf16[16,64,224]{2,1,0:T(8,128)(2,1)S(1)} all-to-all(bf16[16,64,224]{2,1,0:T(8,128)(2,1)S(1)} %bitcast.14), channel_id=1, replica_groups=mesh['head_0'=4,'head_1'=2,'expert_0'=8,'expert_1'=2,'expert_2'=2] {'hea..., dimensions={0} | all-to-all | bytes 917504 | tf_op jit(solution)/shard_map/all_to_all | solution.py:455
  106.0 10.5 %all-to-all-start.2 = ((bf16[32,24,224]{2,1,0:T(8,128)(2,1)}), bf16[32,24,224]{2,1,0:T(8,128)(2,1)S(1)}, u32[]{:S(2)}, u32[]{:S(2)}) async-start(bf16[32,24,224]{2,1,0:T(8,128)(2,1)} %copy-done.9), calls=%async_computation.2 | async-start | bytes 786432 | tf_op jit(solution)/shard_map/all_to_all | solution.py:455
  116.6 15.0 %all-to-all-done.2.x_ref = bf16[32,24,224]{2,1,0:T(8,128)(2,1)S(1)} async-done(((bf16[32,24,224]{2,1,0:T(8,128)(2,1)}), bf16[32,24,224]{2,1,0:T(8,128)(2,1)S(1)}, u32[]{:S(2)}, u32[]{:S(2)}) %all-to-all-start.2) | async-done | bytes 344096 | tf_op jit(solution)/shard_map/all_to_all | solution.py:455
  133.9 6.1 %collective-permute-done.21.refs_4_ = bf16[24,7168]{1,0:T(8,128)(2,1)S(1)} collective-permute-done((bf16[24,7168]{1,0:T(8,128)(2,1)S(1)}, bf16[24,7168]{1,0:T(8,128)(2,1)S(1)}, u32[]{:S(2)}, u32[]{:S(2)}) %collective-permute-start.21) | collective-permute-done | bytes 344096 | tf_op jit(solution)/shard_map/ppermute | solution.py:34
  142.8 2.7 %collective-permute-done.22.refs_3_ = bf16[24,3584]{1,0:T(8,128)(2,1)S(1)} collective-permute-done((bf16[24,3584]{1,0:T(8,128)(2,1)S(1)}, bf16[24,3584]{1,0:T(8,128)(2,1)S(1)}, u32[]{:S(2)}, u32[]{:S(2)}) %collective-permute-start.22) | collective-permute-done | bytes 172064 | tf_op jit(solution)/shard_map/ppermute | solution.py:34
  145.5 3.3 %collective-permute-done.20.refs_2_ = bf16[24,3584]{1,0:T(8,128)(2,1)S(1)} collective-permute-done((bf16[24,3584]{1,0:T(8,128)(2,1)S(1)}, bf16[24,3584]{1,0:T(8,128)(2,1)S(1)}, u32[]{:S(2)}, u32[]{:S(2)}) %collective-permute-start.20) | collective-permute-done | bytes 172064 | tf_op jit(solution)/shard_map/ppermute | solution.py:34
  155.4 2.3 %collective-permute-done.30.refs_3_ = bf16[192,128]{1,0:T(8,128)(2,1)S(1)} collective-permute-done((bf16[192,128]{1,0:T(8,128)(2,1)S(1)}, bf16[192,128]{1,0:T(8,128)(2,1)S(1)}, u32[]{:S(2)}, u32[]{:S(2)}) %collective-permute-start.30) | collective-permute-done | bytes 49184 | tf_op jit(solution)/shard_map/ppermute | solution.py:34
  166.8 3.0 %collective-permute-done.32.refs_1_ = bf16[24,1792]{1,0:T(8,128)(2,1)S(1)} collective-permute-done((bf16[24,1792]{1,0:T(8,128)(2,1)S(1)}, bf16[24,1792]{1,0:T(8,128)(2,1)S(1)}, u32[]{:S(2)}, u32[]{:S(2)}) %collective-permute-start.32) | collective-permute-done | bytes 86048 | tf_op jit(solution)/shard_map/ppermute | solution.py:34
  169.8 2.8 %collective-permute-done.33.refs_2_ = bf16[24,1792]{1,0:T(8,128)(2,1)S(1)} collective-permute-done((bf16[24,1792]{1,0:T(8,128)(2,1)S(1)}, bf16[24,1792]{1,0:T(8,128)(2,1)S(1)}, u32[]{:S(2)}, u32[]{:S(2)}) %collective-permute-start.33) | collective-permute-done | bytes 86048 | tf_op jit(solution)/shard_map/ppermute | solution.py:34
  174.2 19.8 %all_to_all.21.back_ref = bf16[32,24,224]{2,1,0:T(8,128)(2,1)S(1)} all-to-all(bf16[32,24,224]{2,1,0:T(8,128)(2,1)S(1)} %by_columns.1), channel_id=1, replica_groups=mesh['head_0'=4,'head_1'=2,'expert_0'=8,'expert_1'=2,'expert_2'=2] {'exp..., dimensions={0} | all-to-all | bytes 688128 | tf_op jit(solution)/shard_map/all_to_all | solution.py:455
  (124 shorter events, 62.4 us)
Async XLA Ops:
  3.3 31.8 %all-to-all-start = ((bf16[32,16,576]{2,1,0:T(8,128)(2,1)}), bf16[32,16,576]{2,1,0:T(8,128)(2,1)S(1)}, u32[]{:S(2)}, u32[]{:S(2)}) async-start(bf16[32,16,576]{2,1,0:T(8,128)(2,1)} %pack_cache.1), calls=%async_computation | async-start | bytes 1310720 | tf_op jit(solution)/shard_map/all_to_all | solution.py:455
  17.0 17.3 %collective-permute-start = (bf16[224,1024]{1,0:T(8,128)(2,1)}, bf16[224,1024]{1,0:T(8,128)(2,1)}, u32[]{:S(2)}, u32[]{:S(2)}) collective-permute-start(bf16[224,1024]{1,0:T(8,128)(2,1)} %get-tuple-element.89), channel_id=1, source_target_pairs={{0,1},{1,0},{2,3},{3,2},{4,5},{5,4},{6,7},{7,6},{8,9},{9,8},{10,11... | collective-permute-start | bytes 1376264 | tf_op jit(solution)/shard_map/ppermute | solution.py:38
  19.6 14.7 %collective-permute-start.2 = (bf16[128,1792]{1,0:T(8,128)(2,1)}, bf16[128,1792]{1,0:T(8,128)(2,1)}, u32[]{:S(2)}, u32[]{:S(2)}) collective-permute-start(bf16[128,1792]{1,0:T(8,128)(2,1)} %get-tuple-element.85), channel_id=1, source_target_pairs={{0,192},{64,0},{128,64},{192,128},{1,193},{65,1},{129,65},{193,129... | collective-permute-start | bytes 1376264 | tf_op jit(solution)/shard_map/ppermute | solution.py:34
  22.4 12.7 %collective-permute-start.1 = (bf16[128,1792]{1,0:T(8,128)(2,1)}, bf16[128,1792]{1,0:T(8,128)(2,1)}, u32[]{:S(2)}, u32[]{:S(2)}) collective-permute-start(bf16[128,1792]{1,0:T(8,128)(2,1)} %get-tuple-element.87), channel_id=1, source_target_pairs={{0,64},{64,128},{128,192},{192,0},{1,65},{65,129},{129,193},{193,1... | collective-permute-start | bytes 1376264 | tf_op jit(solution)/shard_map/ppermute | solution.py:34
  35.9 6.4 %collective-permute-start.6 = (bf16[6,16,576]{2,1,0:T(8,128)(2,1)S(1)}, bf16[6,16,576]{2,1,0:T(8,128)(2,1)S(1)}, u32[]{:S(2)}, u32[]{:S(2)}) collective-permute-start(bf16[6,16,576]{2,1,0:T(8,128)(2,1)S(1)} %select_arrived.1.refs_0_), channel_id=1, source_target_pairs={{0,192},{64,0},{128,64},{192,128},{1,193},{65,1},{129,65},{193,129... | collective-permute-start | bytes 331784 | tf_op jit(solution)/shard_map/ppermute | solution.py:34
  38.2 6.5 %collective-permute-start.5 = (bf16[6,16,576]{2,1,0:T(8,128)(2,1)S(1)}, bf16[6,16,576]{2,1,0:T(8,128)(2,1)S(1)}, u32[]{:S(2)}, u32[]{:S(2)}) collective-permute-start(bf16[6,16,576]{2,1,0:T(8,128)(2,1)S(1)} %select_arrived.1.refs_0_), channel_id=1, source_target_pairs={{0,128},{64,192},{128,0},{192,64},{1,129},{65,193},{129,1},{193,65... | collective-permute-start | bytes 331784 | tf_op jit(solution)/shard_map/ppermute | solution.py:34
  39.0 6.9 %collective-permute-start.4 = (bf16[6,16,576]{2,1,0:T(8,128)(2,1)S(1)}, bf16[6,16,576]{2,1,0:T(8,128)(2,1)S(1)}, u32[]{:S(2)}, u32[]{:S(2)}) collective-permute-start(bf16[6,16,576]{2,1,0:T(8,128)(2,1)S(1)} %select_arrived.1.refs_0_), channel_id=1, source_target_pairs={{0,64},{64,128},{128,192},{192,0},{1,65},{65,129},{129,193},{193,1... | collective-permute-start | bytes 331784 | tf_op jit(solution)/shard_map/ppermute | solution.py:34
  65.8 16.7 %collective-permute-start.3 = (bf16[128,1792]{1,0:T(8,128)(2,1)}, bf16[128,1792]{1,0:T(8,128)(2,1)S(1)}, u32[]{:S(2)}, u32[]{:S(2)}) collective-permute-start(bf16[128,1792]{1,0:T(8,128)(2,1)} %get-tuple-element.49), channel_id=1, source_target_pairs={{0,128},{64,192},{128,0},{192,64},{1,129},{65,193},{129,1},{193,65... | collective-permute-start | bytes 1376264 | tf_op jit(solution)/shard_map/ppermute | solution.py:34
  69.5 6.2 %collective-permute-start.12 = (bf16[64,1024]{1,0:T(8,128)(2,1)S(1)}, bf16[64,1024]{1,0:T(8,128)(2,1)S(1)}, u32[]{:S(2)}, u32[]{:S(2)}) collective-permute-start(bf16[64,1024]{1,0:T(8,128)(2,1)S(1)} %collective-permute-done.11.refs_1_), channel_id=1, source_target_pairs={{0,4},{4,8},{8,12},{12,16},{16,20},{20,24},{24,28},{28,0},{1,5},{5... | collective-permute-start | bytes 393224 | tf_op jit(solution)/shard_map/ppermute | solution.py:34
  73.0 5.7 %collective-permute-start.17 = (bf16[64,1024]{1,0:T(8,128)(2,1)S(1)}, bf16[64,1024]{1,0:T(8,128)(2,1)S(1)}, u32[]{:S(2)}, u32[]{:S(2)}) collective-permute-start(bf16[64,1024]{1,0:T(8,128)(2,1)S(1)} %collective-permute-done.16.refs_7_), channel_id=1, source_target_pairs={{0,28},{4,0},{8,4},{12,8},{16,12},{20,16},{24,20},{28,24},{1,29},{... | collective-permute-start | bytes 393224 | tf_op jit(solution)/shard_map/ppermute | solution.py:34
  75.7 6.7 %collective-permute-start.13 = (bf16[64,1024]{1,0:T(8,128)(2,1)S(1)}, bf16[64,1024]{1,0:T(8,128)(2,1)S(1)}, u32[]{:S(2)}, u32[]{:S(2)}) collective-permute-start(bf16[64,1024]{1,0:T(8,128)(2,1)S(1)} %collective-permute-done.12.refs_2_), channel_id=1, source_target_pairs={{0,4},{4,8},{8,12},{12,16},{16,20},{20,24},{24,28},{28,0},{1,5},{5... | collective-permute-start | bytes 393224 | tf_op jit(solution)/shard_map/ppermute | solution.py:34
  78.7 5.8 %collective-permute-start.18 = (bf16[32,1024]{1,0:T(8,128)(2,1)S(1)}, bf16[32,1024]{1,0:T(8,128)(2,1)S(1)}, u32[]{:S(2)}, u32[]{:S(2)}) collective-permute-start(bf16[32,1024]{1,0:T(8,128)(2,1)S(1)} %slice.30), channel_id=1, source_target_pairs={{0,28},{4,0},{8,4},{12,8},{16,12},{20,16},{24,20},{28,24},{1,29},{... | collective-permute-start | bytes 196616 | tf_op jit(solution)/shard_map/ppermute | solution.py:34
  106.0 25.5 %all-to-all-start.2 = ((bf16[32,24,224]{2,1,0:T(8,128)(2,1)}), bf16[32,24,224]{2,1,0:T(8,128)(2,1)S(1)}, u32[]{:S(2)}, u32[]{:S(2)}) async-start(bf16[32,24,224]{2,1,0:T(8,128)(2,1)} %copy-done.9), calls=%async_computation.2 | async-start | bytes 786432 | tf_op jit(solution)/shard_map/all_to_all | solution.py:455
  131.8 8.2 %collective-permute-start.21 = (bf16[24,7168]{1,0:T(8,128)(2,1)S(1)}, bf16[24,7168]{1,0:T(8,128)(2,1)S(1)}, u32[]{:S(2)}, u32[]{:S(2)}) collective-permute-start(bf16[24,7168]{1,0:T(8,128)(2,1)S(1)} %norm.1.refs_0_), channel_id=1, source_target_pairs={{0,192},{64,0},{128,64},{192,128},{1,193},{65,1},{129,65},{193,129... | collective-permute-start | bytes 1032200 | tf_op jit(solution)/shard_map/ppermute | solution.py:34
  132.3 9.8 %collective-permute-start.19 = (bf16[24,7168]{1,0:T(8,128)(2,1)S(1)}, bf16[24,7168]{1,0:T(8,128)(2,1)S(1)}, u32[]{:S(2)}, u32[]{:S(2)}) collective-permute-start(bf16[24,7168]{1,0:T(8,128)(2,1)S(1)} %norm.1.refs_0_), channel_id=1, source_target_pairs={{0,64},{64,128},{128,192},{192,0},{1,65},{65,129},{129,193},{193,1... | collective-permute-start | bytes 1032200 | tf_op jit(solution)/shard_map/ppermute | solution.py:34
  133.9 14.9 %collective-permute-start.23 = (bf16[24,7168]{1,0:T(8,128)(2,1)S(1)}, bf16[24,7168]{1,0:T(8,128)(2,1)S(1)}, u32[]{:S(2)}, u32[]{:S(2)}) collective-permute-start(bf16[24,7168]{1,0:T(8,128)(2,1)S(1)} %norm.1.refs_0_), channel_id=1, source_target_pairs={{0,32},{32,0},{1,33},{33,1},{2,34},{34,2},{3,35},{35,3},{4,36},{36... | collective-permute-start | bytes 1032200 | tf_op jit(solution)/shard_map/ppermute | solution.py:34
  142.1 6.7 %collective-permute-start.20 = (bf16[24,3584]{1,0:T(8,128)(2,1)S(1)}, bf16[24,3584]{1,0:T(8,128)(2,1)S(1)}, u32[]{:S(2)}, u32[]{:S(2)}) collective-permute-start(bf16[24,3584]{1,0:T(8,128)(2,1)S(1)} %slice.31), channel_id=1, source_target_pairs={{0,64},{64,128},{128,192},{192,0},{1,65},{65,129},{129,193},{193,1... | collective-permute-start | bytes 516104 | tf_op jit(solution)/shard_map/ppermute | solution.py:34
  142.2 6.6 %collective-permute-start.27 = (bf16[24,7168]{1,0:T(8,128)(2,1)S(1)}, bf16[24,7168]{1,0:T(8,128)(2,1)S(1)}, u32[]{:S(2)}, u32[]{:S(2)}) collective-permute-start(bf16[24,7168]{1,0:T(8,128)(2,1)S(1)} %collective-permute-done.21.refs_4_), channel_id=1, source_target_pairs={{0,32},{32,0},{1,33},{33,1},{2,34},{34,2},{3,35},{35,3},{4,36},{36... | collective-permute-start | bytes 1032200 | tf_op jit(solution)/shard_map/ppermute | solution.py:34
  142.3 7.9 %collective-permute-start.24 = (bf16[24,7168]{1,0:T(8,128)(2,1)S(1)}, bf16[24,7168]{1,0:T(8,128)(2,1)S(1)}, u32[]{:S(2)}, u32[]{:S(2)}) collective-permute-start(bf16[24,7168]{1,0:T(8,128)(2,1)S(1)} %collective-permute-done.19.refs_1_), channel_id=1, source_target_pairs={{0,32},{32,0},{1,33},{33,1},{2,34},{34,2},{3,35},{35,3},{4,36},{36... | collective-permute-start | bytes 1032200 | tf_op jit(solution)/shard_map/ppermute | solution.py:34
  153.6 5.7 %collective-permute-start.29 = (bf16[192,128]{1,0:T(8,128)(2,1)S(1)}, bf16[192,128]{1,0:T(8,128)(2,1)S(1)}, u32[]{:S(2)}, u32[]{:S(2)}) collective-permute-start(bf16[192,128]{1,0:T(8,128)(2,1)S(1)} %units.1.refs_0_), channel_id=1, source_target_pairs={{0,128},{64,192},{128,0},{192,64},{1,129},{65,193},{129,1},{193,65... | collective-permute-start | bytes 147464 | tf_op jit(solution)/shard_map/ppermute | solution.py:34
  154.3 5.9 %collective-permute-start.28 = (bf16[192,128]{1,0:T(8,128)(2,1)S(1)}, bf16[192,128]{1,0:T(8,128)(2,1)S(1)}, u32[]{:S(2)}, u32[]{:S(2)}) collective-permute-start(bf16[192,128]{1,0:T(8,128)(2,1)S(1)} %units.1.refs_0_), channel_id=1, source_target_pairs={{0,64},{64,128},{128,192},{192,0},{1,65},{65,129},{129,193},{193,1... | collective-permute-start | bytes 147464 | tf_op jit(solution)/shard_map/ppermute | solution.py:34
  163.7 6.1 %collective-permute-start.32 = (bf16[24,1792]{1,0:T(8,128)(2,1)S(1)}, bf16[24,1792]{1,0:T(8,128)(2,1)S(1)}, u32[]{:S(2)}, u32[]{:S(2)}) collective-permute-start(bf16[24,1792]{1,0:T(8,128)(2,1)S(1)} %get-tuple-element.78), channel_id=1, source_target_pairs={{0,192},{64,0},{128,64},{192,128},{1,193},{65,1},{129,65},{193,129... | collective-permute-start | bytes 258056 | tf_op jit(solution)/shard_map/ppermute | solution.py:34
  165.8 6.7 %collective-permute-start.33 = (bf16[24,1792]{1,0:T(8,128)(2,1)S(1)}, bf16[24,1792]{1,0:T(8,128)(2,1)S(1)}, u32[]{:S(2)}, u32[]{:S(2)}) collective-permute-start(bf16[24,1792]{1,0:T(8,128)(2,1)S(1)} %get-tuple-element.79), channel_id=1, source_target_pairs={{0,128},{64,192},{128,0},{192,64},{1,129},{65,193},{129,1},{193,65... | collective-permute-start | bytes 258056 | tf_op jit(solution)/shard_map/ppermute | solution.py:34
  166.7 6.7 %collective-permute-start.34 = (bf16[24,1792]{1,0:T(8,128)(2,1)S(1)}, bf16[24,1792]{1,0:T(8,128)(2,1)S(1)}, u32[]{:S(2)}, u32[]{:S(2)}) collective-permute-start(bf16[24,1792]{1,0:T(8,128)(2,1)S(1)} %get-tuple-element.80), channel_id=1, source_target_pairs={{0,64},{64,128},{128,192},{192,0},{1,65},{65,129},{129,193},{193,1... | collective-permute-start | bytes 258056 | tf_op jit(solution)/shard_map/ppermute | solution.py:34
  (29 other events, 282.7 us)

commit v2 on v0

--- a/solution.py
+++ b/solution.py
@@ -168,7 +168,7 @@
     each = heads // groups
     for d, out_ref in enumerate(out_refs):
         for k in range(each):
-            h = lax.rem(row + d, groups) * each + k
+            h = k if groups == 1 else lax.rem(row + d, groups) * each + k
             values = jnp.dot(latents[h].astype(BF), up_ref[h], preferred_element_type=F32)
             rows = jnp.concatenate([res_ref[h].astype(F32), values[:count]], axis=0).astype(BF)
             out_ref[:, k * value_width : (k + 1) * value_width] = rows
@@ -207,25 +207,24 @@
     )(*pieces)
 
 
-def project_kernel(count, places, *refs):
-    pieces, weights, out_ref = refs[:count], refs[count:-1], refs[-1]
-    rows = out_ref.shape[2]
+def project_kernel(makers, w_ref, *refs):
+    pieces, out_ref = refs[:-1], refs[-1]
+    rows = out_ref.shape[1]
     attention = jnp.concatenate([piece[...] for piece in pieces], axis=0)
-    for q, w in enumerate(weights):
-        mixed = lax.dot_general(attention, w[...], (((1,), (1,)), ((), ())), preferred_element_type=F32).astype(BF)
-        for k in range(attention.shape[0] // rows):
-            out_ref[places[q, k], places[2, k]] = mixed[k * rows : (k + 1) * rows]
-
-
-def project(places, pieces, weights, shape):
-    return pl.pallas_call(
-        functools.partial(project_kernel, len(pieces)),
-        out_shape=jax.ShapeDtypeStruct(shape, BF),
-        in_specs=[whole(pltpu.SMEM)] + [whole()] * (len(pieces) + len(weights)),
+    mixed = lax.dot_general(attention, w_ref[...], (((1,), (1,)), ((), ())), preferred_element_type=F32).astype(BF)
+    for k in range(out_ref.shape[0]):
+        out_ref[makers[k]] = mixed[k * rows : (k + 1) * rows]
+
+
+def project(makers, w_output_t, pieces, rows):
+    return pl.pallas_call(
+        project_kernel,
+        out_shape=jax.ShapeDtypeStruct((makers.shape[0], rows, w_output_t.shape[0]), BF),
+        in_specs=[whole(pltpu.SMEM)] + [whole()] * (1 + len(pieces)),
         out_specs=whole(),
         compiler_params=params(),
         name="project",
-    )(places, *pieces, *weights)
+    )(makers, w_output_t, *pieces)
 
 
 def pair_kernel(a_ref, b_ref, *outs):
@@ -492,35 +491,30 @@
 
     packed = pack_cache(new_owner, new_cache, new_cache.shape[1] // ring, n_expert)
     resident = attend(queries[:req_count], jnp.swapaxes(resident_cache, 1, 2), resident_len, value_up)
-    arrived, resident = lax.optimization_barrier((exchange(packed, EXPERT), resident))
+
+    packed, w_d = lax.optimization_barrier((packed, w_down.reshape(w_down.shape[1:])))
+    part = w_d.shape[1] // ring
+    downs = [lax.dynamic_slice_in_dim(w_d, ((x + d) % ring) * part, part, 1) for d in range(ring)]
+    for d in (1, 3):
+        downs[d] = shifted(downs[d], HEAD[0], d)
+    arrived, resident, downs = lax.optimization_barrier((exchange(packed, EXPERT), resident, downs))
     ours = select_arrived(sources, arrived)
     near = [ours] + [shifted(ours, HEAD[0], d) for d in range(1, ring)]
     pieces = near + [shifted(p, HEAD[1], 1) for p in near]
-    attention = new_attention(lens, at, queries, value_up, resident, pieces, 2)
-
-    w_t = w_output.T
-    width = w_t.shape[1] // 2
-    group = lambda d: lax.dynamic_slice_in_dim(w_t, ((y + d) % 2) * width, width, 1)
-    weights = [group(0), across(group(1), COLUMN, 1)]
-    along_y = list(attention[:1]) + [across(attention[d % 2], COLUMN, d) for d in range(1, n_y)]
+    (attention,) = new_attention(lens, at, queries, value_up, resident, pieces, 1)
+
+    along_y = [attention] + [across(attention, COLUMN, d) for d in range(1, n_y)]
     rows_here = flat(ring_gather(stacked(along_y), EXPERT[0], 0))
-    w_d = w_down.reshape(w_down.shape[1:])
-    part = w_d.shape[1] // ring
-    some = lambda d: lax.dynamic_slice_in_dim(w_d, ((x + d) % ring) * part, part, 1)
-    downs = [some(0)] + [shifted(some(d), HEAD[0], d) for d in range(1, ring)]
-    downs, rows_here = lax.optimization_barrier((downs, rows_here))
+    downs[2] = shifted(downs[2], HEAD[0], 2)
+    block = lambda a: lax.dynamic_slice_in_dim(a, head * block_rows, block_rows)
+    planned = plan(block(expert_ids), block(expert_gates), rows_dev, n_expert)
+    downs, rows_here, (sel, mix), kept = lax.optimization_barrier((downs, rows_here, planned, block(residual)))
     away = jnp.arange(n_expert, dtype=I32)
     maker_z = (z + n_z - away // n_y) % n_z
     maker_y = y ^ (away % n_y)
-    per_head = n_expert // n_head
-    maker_head = (maker_z * n_y + maker_y) // per_head
-    places = jnp.stack([maker_head * 2 + y % 2, maker_head * 2 + (y + 1) % 2, (maker_z * n_y + maker_y) % per_head])
-    mixed = project(places, rows_here, weights, (2 * n_head, per_head, rows_dev, columns))
-    parts = exchange(mixed.reshape(2 * n_head, block_rows, columns), HEAD + COLUMN[1:])
-
-    block = lambda a: lax.dynamic_slice_in_dim(a, head * block_rows, block_rows)
-    sel, mix = plan(block(expert_ids), block(expert_gates), rows_dev, n_expert)
-    hidden, outgoing = dispatch(parts, block(residual), sel, n_expert)
+    mixed = project(maker_z * n_y + maker_y, w_output.T, rows_here, rows_dev)
+    parts = exchange(mixed.reshape(n_head, block_rows, columns), HEAD)
+    hidden, outgoing = dispatch(parts, kept, sel, n_expert)
     received = exchange(outgoing, EXPERT)
     normed = normed_rows(received, norm_gain.reshape(1, -1))
     layout, pieces = gather_over_head(normed)

time: 199 us -> 194 us (0.975)
  blocking collectives: 19.8 us -> 30.4 us
  waiting for transfers between devices: 82.8 us -> 73.6 us
  starting transfers between devices: 57.2 us -> 51.5 us
  local copies, waits for them, and re-layouts: 18.6 us -> 15.2 us
    all_to_all x3 -> x2, waiting for transfers between devices: 32.9 us -> 16.4 us  [exchange(): return lax.all_to_all(x, axes, split_axis=0, concat_axis=0, tiled=True)]
    all_to_all x1 -> x2, blocking collectives: 19.8 us -> 30.4 us  [exchange(): return lax.all_to_all(x, axes, split_axis=0, concat_axis=0, tiled=True)]
    ppermute x34, waiting for transfers between devices: 46.2 us -> 53.3 us  [shifted(): return lax.ppermute(x, axis, [(i, (i + step) % n) for i in range(n)])]
    all_to_all x3 -> x2, starting transfers between devices: 25.7 us -> 21 us  [exchange(): return lax.all_to_all(x, axes, split_axis=0, concat_axis=0, tiled=True)]
    unnamed x49 -> x36, local copies, waits for them, and re-layouts: 10.8 us -> 8.75 us
    dynamic_slice x1 -> x0, local copies, waits for them, and re-layouts: 2 us -> none  [per_device(): lax.dynamic_slice_in_dim(w_t, (y + d) % 2 * width, width, 1)]
    ppermute x4 -> x3, starting transfers between devices: 3.58 us -> 4.18 us  [across(): lax.ppermute(x, axis, [(i, i ^ mask) for i in range(lax.axis_size(axis))])]
  transfers between devices with their start and end apart: 41 -> 39, of which waited for: 25 -> 25; matrix products, arithmetic and copies ran while one was open for 7% -> 7% of each run, Pallas kernels for 0% -> 0%
where the time goes in v2:
time: 194 us; the launch traced here: 193 us
  waiting for transfers between devices  73.6 us (38%)
  starting transfers between devices  51.5 us (27%)
  blocking collectives  30.4 us (16%)
  Pallas kernels  16.4 us (8%)
  local copies, waits for them, and re-layouts  15.2 us (8%)
  matrix products  5.08 us (3%)
    ppermute x34, waiting for transfers between devices, shifted(): return lax.ppermute(x, axis, [(i, (i + step) % n) for i in range(n)])  53.3 us
    all_to_all x2, blocking collectives, exchange(): return lax.all_to_all(x, axes, split_axis=0, concat_axis=0, tiled=True)  30.4 us
    ppermute x34, starting transfers between devices, shifted(): return lax.ppermute(x, axis, [(i, (i + step) % n) for i in range(n)])  26.4 us
    all_to_all x2, starting transfers between devices, exchange(): return lax.all_to_all(x, axes, split_axis=0, concat_axis=0, tiled=True)  21 us
    all_to_all x2, waiting for transfers between devices, exchange(): return lax.all_to_all(x, axes, split_axis=0, concat_axis=0, tiled=True)  16.4 us
    unnamed x36, local copies, waits for them, and re-layouts  8.75 us
    pallas_call x1, Pallas kernels, new_attention(): pl.pallas_call(functools.partial(new_attention_kernel, groups), out_shape...  5.54 us
    ppermute x3, starting transfers between devices, across(): lax.ppermute(x, axis, [(i, i ^ mask) for i in range(lax.axis_size(axis))])  4.18 us
  transfers between devices with their start and end apart: 39, of which 25 were waited for; matrix products, arithmetic and copies ran while one was open for 7% of the time, Pallas kernels for 0%

profile of v2, /device:TPU:32, one launch (start us, length us, event | category | flops | bytes accessed | tf_op | source)
XLA Modules:
  0.0 193.3 jit_solution(7570539705955989963)
XLA Ops:
  3.3 11.4 %all-to-all-start = ((bf16[32,16,576]{2,1,0:T(8,128)(2,1)}), bf16[32,16,576]{2,1,0:T(8,128)(2,1)S(1)}, u32[]{:S(2)}, u32[]{:S(2)}) async-start(bf16[32,16,576]{2,1,0:T(8,128)(2,1)} %pack_cache.1), calls=%async_computation | async-start | bytes 1310720 | tf_op jit(solution)/shard_map/all_to_all | solution.py:439
  15.9 2.8 %collective-permute-start.1 = (bf16[128,1792]{1,0:T(8,128)(2,1)}, bf16[128,1792]{1,0:T(8,128)(2,1)}, u32[]{:S(2)}, u32[]{:S(2)}) collective-permute-start(bf16[128,1792]{1,0:T(8,128)(2,1)} %get-tuple-element.75), channel_id=1, source_target_pairs={{0,192},{64,0},{128,64},{192,128},{1,193},{65,1},{129,65},{193,129... | collective-permute-start | bytes 1376264 | tf_op jit(solution)/shard_map/ppermute | solution.py:34
  21.0 2.3 %fusion.4 = bf16[4,16,512]{2,1,0:T(8,128)(2,1)} fusion(bf16[4,576,256]{2,1,0:T(8,128)(2,1)} %bitcast.19, f32[4,16]{1,0:T(4,128)S(1)} %fusion.18, f32[4,16,256]{2,1,0:T(8,128)S(1)} %fusion.2), kind=kOutput, calls=%fused_computation.6 | convolution fusion | flops 16826688 | bytes 1247232 | tf_op jit(solution)/shard_map/rht,rct->rhc/dot_general | solution.py:72
  24.4 3.8 %collective-permute-done.1.refs_7_ = bf16[128,1792]{1,0:T(8,128)(2,1)} collective-permute-done((bf16[128,1792]{1,0:T(8,128)(2,1)}, bf16[128,1792]{1,0:T(8,128)(2,1)}, u32[]{:S(2)}, u32[]{:S(2)}) %collective-permute-start.1) | collective-permute-done | bytes 458784 | tf_op jit(solution)/shard_map/ppermute | solution.py:34
  28.2 3.4 %collective-permute-done.refs_5_ = bf16[128,1792]{1,0:T(8,128)(2,1)} collective-permute-done((bf16[128,1792]{1,0:T(8,128)(2,1)}, bf16[128,1792]{1,0:T(8,128)(2,1)}, u32[]{:S(2)}, u32[]{:S(2)}) %collective-permute-start) | collective-permute-done | bytes 458784 | tf_op jit(solution)/shard_map/ppermute | solution.py:34
  31.7 2.8 %all-to-all-done.arrived_ref = bf16[32,16,576]{2,1,0:T(8,128)(2,1)S(1)} async-done(((bf16[32,16,576]{2,1,0:T(8,128)(2,1)}), bf16[32,16,576]{2,1,0:T(8,128)(2,1)S(1)}, u32[]{:S(2)}, u32[]{:S(2)}) %all-to-all-start) | async-done | bytes 589856 | tf_op jit(solution)/shard_map/all_to_all | solution.py:439
  35.7 2.8 %collective-permute-start.5 = (bf16[6,16,576]{2,1,0:T(8,128)(2,1)}, bf16[6,16,576]{2,1,0:T(8,128)(2,1)S(1)}, u32[]{:S(2)}, u32[]{:S(2)}) collective-permute-start(bf16[6,16,576]{2,1,0:T(8,128)(2,1)} %select_arrived.1.refs_0_), channel_id=1, source_target_pairs={{0,192},{64,0},{128,64},{192,128},{1,193},{65,1},{129,65},{193,129... | collective-permute-start | bytes 331784 | tf_op jit(solution)/shard_map/ppermute | solution.py:34
  41.3 3.9 %collective-permute-done.4.refs_2_ = bf16[6,16,576]{2,1,0:T(8,128)(2,1)S(1)} collective-permute-done((bf16[6,16,576]{2,1,0:T(8,128)(2,1)}, bf16[6,16,576]{2,1,0:T(8,128)(2,1)S(1)}, u32[]{:S(2)}, u32[]{:S(2)}) %collective-permute-start.4) | collective-permute-done | bytes 110624 | tf_op jit(solution)/shard_map/ppermute | solution.py:34
  48.8 5.5 %new_attention.1.refs_0_ = bf16[16,2048]{1,0:T(8,128)(2,1)S(1)} custom-call(s32[12]{0:T(128)S(1)} %get-tuple-element.74.lens, s32[3]{0:T(128)S(1)} %pad_add_fusion.at, bf16[16,16,576]{2,1,0:T(8,128)(2,1)S(1)} %copy-done.5, bf16[16,512,128]{2,1,0:T(8,128)(2,1)S(1)} %copy-done.1, bf16[16,4,128]{2,1,0:T(4,128)(2,1)S(1)} %convolution_convert_fusion.res_ref, ...), custom_call_target="tpu_custom_call" | custom-call | tf_op jit(solution)/shard_map/new_attention/pallas_call | solution.py:181
  59.9 2.5 %collective-permute-done.11.refs_2_ = bf16[16,2048]{1,0:T(8,128)(2,1)S(1)} collective-permute-done((bf16[16,2048]{1,0:T(8,128)(2,1)S(1)}, bf16[16,2048]{1,0:T(8,128)(2,1)S(1)}, u32[]{:S(2)}, u32[]{:S(2)}) %collective-permute-start.11) | collective-permute-done | bytes 65568 | tf_op jit(solution)/shard_map/ppermute | solution.py:38
  64.6 4.6 %collective-permute-done.17.refs_8_ = bf16[64,2048]{1,0:T(8,128)(2,1)S(1)} collective-permute-done((bf16[64,2048]{1,0:T(8,128)(2,1)S(1)}, bf16[64,2048]{1,0:T(8,128)(2,1)S(1)}, u32[]{:S(2)}, u32[]{:S(2)}) %collective-permute-start.17) | collective-permute-done | bytes 262176 | tf_op jit(solution)/shard_map/ppermute | solution.py:34
  71.2 4.9 %collective-permute-done.18.refs_7_ = bf16[64,2048]{1,0:T(8,128)(2,1)} collective-permute-done((bf16[64,2048]{1,0:T(8,128)(2,1)S(1)}, bf16[64,2048]{1,0:T(8,128)(2,1)}, u32[]{:S(2)}, u32[]{:S(2)}) %collective-permute-start.18) | collective-permute-done | bytes 262176 | tf_op jit(solution)/shard_map/ppermute | solution.py:34
  80.7 2.3 %collective-permute-done.19.refs_6_ = bf16[64,2048]{1,0:T(8,128)(2,1)S(1)} collective-permute-done((bf16[64,2048]{1,0:T(8,128)(2,1)}, bf16[64,2048]{1,0:T(8,128)(2,1)S(1)}, u32[]{:S(2)}, u32[]{:S(2)}) %collective-permute-start.19) | collective-permute-done | bytes 262176 | tf_op jit(solution)/shard_map/ppermute | solution.py:34
  83.6 2.0 %collective-permute-start.20 = (bf16[32,2048]{1,0:T(8,128)(2,1)}, bf16[32,2048]{1,0:T(8,128)(2,1)S(1)}, u32[]{:S(2)}, u32[]{:S(2)}) collective-permute-start(bf16[32,2048]{1,0:T(8,128)(2,1)} %slice.30), channel_id=1, source_target_pairs={{0,28},{4,0},{8,4},{12,8},{16,12},{20,16},{24,20},{28,24},{1,29},{... | collective-permute-start | bytes 393224 | tf_op jit(solution)/shard_map/ppermute | solution.py:34
  94.1 10.1 %all_to_all.20.parts_ref = bf16[8,64,224]{2,1,0:T(8,128)(2,1)S(1)} all-to-all(bf16[8,64,224]{2,1,0:T(8,128)(2,1)S(1)} %bitcast.16), channel_id=1, replica_groups=mesh['head_0'=4,'head_1'=2,'expert_0'=8,'expert_1'=2,'expert_2'=2] {'hea..., dimensions={0} | all-to-all | bytes 458752 | tf_op jit(solution)/shard_map/all_to_all | solution.py:439
  105.2 9.6 %all-to-all-start.2 = ((bf16[32,24,224]{2,1,0:T(8,128)(2,1)}), bf16[32,24,224]{2,1,0:T(8,128)(2,1)S(1)}, u32[]{:S(2)}, u32[]{:S(2)}) async-start(bf16[32,24,224]{2,1,0:T(8,128)(2,1)} %copy-done.7), calls=%async_computation.2 | async-start | bytes 786432 | tf_op jit(solution)/shard_map/all_to_all | solution.py:439
  115.5 13.6 %all-to-all-done.2.x_ref = bf16[32,24,224]{2,1,0:T(8,128)(2,1)S(1)} async-done(((bf16[32,24,224]{2,1,0:T(8,128)(2,1)}), bf16[32,24,224]{2,1,0:T(8,128)(2,1)S(1)}, u32[]{:S(2)}, u32[]{:S(2)}) %all-to-all-start.2) | async-done | bytes 344096 | tf_op jit(solution)/shard_map/all_to_all | solution.py:439
  131.5 6.8 %collective-permute-done.23.refs_4_ = bf16[24,7168]{1,0:T(8,128)(2,1)S(1)} collective-permute-done((bf16[24,7168]{1,0:T(8,128)(2,1)S(1)}, bf16[24,7168]{1,0:T(8,128)(2,1)S(1)}, u32[]{:S(2)}, u32[]{:S(2)}) %collective-permute-start.23) | collective-permute-done | bytes 344096 | tf_op jit(solution)/shard_map/ppermute | solution.py:34
  141.0 2.8 %collective-permute-done.24.refs_3_ = bf16[24,3584]{1,0:T(8,128)(2,1)S(1)} collective-permute-done((bf16[24,3584]{1,0:T(8,128)(2,1)S(1)}, bf16[24,3584]{1,0:T(8,128)(2,1)S(1)}, u32[]{:S(2)}, u32[]{:S(2)}) %collective-permute-start.24) | collective-permute-done | bytes 172064 | tf_op jit(solution)/shard_map/ppermute | solution.py:34
  143.8 2.6 %collective-permute-done.22.refs_2_ = bf16[24,3584]{1,0:T(8,128)(2,1)S(1)} collective-permute-done((bf16[24,3584]{1,0:T(8,128)(2,1)S(1)}, bf16[24,3584]{1,0:T(8,128)(2,1)S(1)}, u32[]{:S(2)}, u32[]{:S(2)}) %collective-permute-start.22) | collective-permute-done | bytes 172064 | tf_op jit(solution)/shard_map/ppermute | solution.py:34
  153.0 2.3 %collective-permute-done.32.refs_3_ = bf16[192,128]{1,0:T(8,128)(2,1)S(1)} collective-permute-done((bf16[192,128]{1,0:T(8,128)(2,1)S(1)}, bf16[192,128]{1,0:T(8,128)(2,1)S(1)}, u32[]{:S(2)}, u32[]{:S(2)}) %collective-permute-start.32) | collective-permute-done | bytes 49184 | tf_op jit(solution)/shard_map/ppermute | solution.py:34
  164.3 3.0 %collective-permute-done.34.refs_1_ = bf16[24,1792]{1,0:T(8,128)(2,1)S(1)} collective-permute-done((bf16[24,1792]{1,0:T(8,128)(2,1)S(1)}, bf16[24,1792]{1,0:T(8,128)(2,1)S(1)}, u32[]{:S(2)}, u32[]{:S(2)}) %collective-permute-start.34) | collective-permute-done | bytes 86048 | tf_op jit(solution)/shard_map/ppermute | solution.py:34
  167.3 2.8 %collective-permute-done.35.refs_2_ = bf16[24,1792]{1,0:T(8,128)(2,1)S(1)} collective-permute-done((bf16[24,1792]{1,0:T(8,128)(2,1)S(1)}, bf16[24,1792]{1,0:T(8,128)(2,1)S(1)}, u32[]{:S(2)}, u32[]{:S(2)}) %collective-permute-start.35) | collective-permute-done | bytes 86048 | tf_op jit(solution)/shard_map/ppermute | solution.py:34
  171.7 20.3 %all_to_all.21.back_ref = bf16[32,24,224]{2,1,0:T(8,128)(2,1)S(1)} all-to-all(bf16[32,24,224]{2,1,0:T(8,128)(2,1)S(1)} %by_columns.1), channel_id=1, replica_groups=mesh['head_0'=4,'head_1'=2,'expert_0'=8,'expert_1'=2,'expert_2'=2] {'exp..., dimensions={0} | all-to-all | bytes 688128 | tf_op jit(solution)/shard_map/all_to_all | solution.py:439
  (126 shorter events, 64.0 us)
Async XLA Ops:
  3.3 31.2 %all-to-all-start = ((bf16[32,16,576]{2,1,0:T(8,128)(2,1)}), bf16[32,16,576]{2,1,0:T(8,128)(2,1)S(1)}, u32[]{:S(2)}, u32[]{:S(2)}) async-start(bf16[32,16,576]{2,1,0:T(8,128)(2,1)} %pack_cache.1), calls=%async_computation | async-start | bytes 1310720 | tf_op jit(solution)/shard_map/all_to_all | solution.py:439
  15.9 12.3 %collective-permute-start.1 = (bf16[128,1792]{1,0:T(8,128)(2,1)}, bf16[128,1792]{1,0:T(8,128)(2,1)}, u32[]{:S(2)}, u32[]{:S(2)}) collective-permute-start(bf16[128,1792]{1,0:T(8,128)(2,1)} %get-tuple-element.75), channel_id=1, source_target_pairs={{0,192},{64,0},{128,64},{192,128},{1,193},{65,1},{129,65},{193,129... | collective-permute-start | bytes 1376264 | tf_op jit(solution)/shard_map/ppermute | solution.py:34
  18.7 13.0 %collective-permute-start = (bf16[128,1792]{1,0:T(8,128)(2,1)}, bf16[128,1792]{1,0:T(8,128)(2,1)}, u32[]{:S(2)}, u32[]{:S(2)}) collective-permute-start(bf16[128,1792]{1,0:T(8,128)(2,1)} %get-tuple-element.77), channel_id=1, source_target_pairs={{0,64},{64,128},{128,192},{192,0},{1,65},{65,129},{129,193},{193,1... | collective-permute-start | bytes 1376264 | tf_op jit(solution)/shard_map/ppermute | solution.py:34
  38.6 6.7 %collective-permute-start.4 = (bf16[6,16,576]{2,1,0:T(8,128)(2,1)}, bf16[6,16,576]{2,1,0:T(8,128)(2,1)S(1)}, u32[]{:S(2)}, u32[]{:S(2)}) collective-permute-start(bf16[6,16,576]{2,1,0:T(8,128)(2,1)} %select_arrived.1.refs_0_), channel_id=1, source_target_pairs={{0,128},{64,192},{128,0},{192,64},{1,129},{65,193},{129,1},{193,65... | collective-permute-start | bytes 331784 | tf_op jit(solution)/shard_map/ppermute | solution.py:34
  39.4 7.1 %collective-permute-start.3 = (bf16[6,16,576]{2,1,0:T(8,128)(2,1)}, bf16[6,16,576]{2,1,0:T(8,128)(2,1)S(1)}, u32[]{:S(2)}, u32[]{:S(2)}) collective-permute-start(bf16[6,16,576]{2,1,0:T(8,128)(2,1)} %select_arrived.1.refs_0_), channel_id=1, source_target_pairs={{0,64},{64,128},{128,192},{192,0},{1,65},{65,129},{129,193},{193,1... | collective-permute-start | bytes 331784 | tf_op jit(solution)/shard_map/ppermute | solution.py:34
  40.3 6.3 %collective-permute-start.6 = (bf16[6,16,576]{2,1,0:T(8,128)(2,1)}, bf16[6,16,576]{2,1,0:T(8,128)(2,1)S(1)}, u32[]{:S(2)}, u32[]{:S(2)}) collective-permute-start(bf16[6,16,576]{2,1,0:T(8,128)(2,1)} %select_arrived.1.refs_0_), channel_id=1, source_target_pairs={{0,32},{32,0},{1,33},{33,1},{2,34},{34,2},{3,35},{35,3},{4,36},{36... | collective-permute-start | bytes 331784 | tf_op jit(solution)/shard_map/ppermute | solution.py:34
  56.4 6.1 %collective-permute-start.11 = (bf16[16,2048]{1,0:T(8,128)(2,1)S(1)}, bf16[16,2048]{1,0:T(8,128)(2,1)S(1)}, u32[]{:S(2)}, u32[]{:S(2)}) collective-permute-start(bf16[16,2048]{1,0:T(8,128)(2,1)S(1)} %new_attention.1.refs_0_), channel_id=1, source_target_pairs={{0,2},{1,3},{2,0},{3,1},{4,6},{5,7},{6,4},{7,5},{8,10},{9,11},{10,... | collective-permute-start | bytes 196616 | tf_op jit(solution)/shard_map/ppermute | solution.py:38
  62.5 6.7 %collective-permute-start.17 = (bf16[64,2048]{1,0:T(8,128)(2,1)S(1)}, bf16[64,2048]{1,0:T(8,128)(2,1)S(1)}, u32[]{:S(2)}, u32[]{:S(2)}) collective-permute-start(bf16[64,2048]{1,0:T(8,128)(2,1)S(1)} %stack.17.refs_0_), channel_id=1, source_target_pairs={{0,28},{4,0},{8,4},{12,8},{16,12},{20,16},{24,20},{28,24},{1,29},{... | collective-permute-start | bytes 786440 | tf_op jit(solution)/shard_map/ppermute | solution.py:34
  63.7 6.6 %collective-permute-start.13 = (bf16[64,2048]{1,0:T(8,128)(2,1)S(1)}, bf16[64,2048]{1,0:T(8,128)(2,1)S(1)}, u32[]{:S(2)}, u32[]{:S(2)}) collective-permute-start(bf16[64,2048]{1,0:T(8,128)(2,1)S(1)} %stack.17.refs_0_), channel_id=1, source_target_pairs={{0,4},{4,8},{8,12},{12,16},{16,20},{20,24},{24,28},{28,0},{1,5},{5... | collective-permute-start | bytes 786440 | tf_op jit(solution)/shard_map/ppermute | solution.py:34
  69.2 6.9 %collective-permute-start.18 = (bf16[64,2048]{1,0:T(8,128)(2,1)S(1)}, bf16[64,2048]{1,0:T(8,128)(2,1)}, u32[]{:S(2)}, u32[]{:S(2)}) collective-permute-start(bf16[64,2048]{1,0:T(8,128)(2,1)S(1)} %collective-permute-done.17.refs_8_), channel_id=1, source_target_pairs={{0,28},{4,0},{8,4},{12,8},{16,12},{20,16},{24,20},{28,24},{1,29},{... | collective-permute-start | bytes 786440 | tf_op jit(solution)/shard_map/ppermute | solution.py:34
  70.3 7.2 %collective-permute-start.14 = (bf16[64,2048]{1,0:T(8,128)(2,1)S(1)}, bf16[64,2048]{1,0:T(8,128)(2,1)}, u32[]{:S(2)}, u32[]{:S(2)}) collective-permute-start(bf16[64,2048]{1,0:T(8,128)(2,1)S(1)} %collective-permute-done.13.refs_1_), channel_id=1, source_target_pairs={{0,4},{4,8},{8,12},{12,16},{16,20},{20,24},{24,28},{28,0},{1,5},{5... | collective-permute-start | bytes 786440 | tf_op jit(solution)/shard_map/ppermute | solution.py:34
  76.1 6.8 %collective-permute-start.19 = (bf16[64,2048]{1,0:T(8,128)(2,1)}, bf16[64,2048]{1,0:T(8,128)(2,1)S(1)}, u32[]{:S(2)}, u32[]{:S(2)}) collective-permute-start(bf16[64,2048]{1,0:T(8,128)(2,1)} %collective-permute-done.18.refs_7_), channel_id=1, source_target_pairs={{0,28},{4,0},{8,4},{12,8},{16,12},{20,16},{24,20},{28,24},{1,29},{... | collective-permute-start | bytes 786440 | tf_op jit(solution)/shard_map/ppermute | solution.py:34
  77.5 8.1 %collective-permute-start.15 = (bf16[64,2048]{1,0:T(8,128)(2,1)}, bf16[64,2048]{1,0:T(8,128)(2,1)S(1)}, u32[]{:S(2)}, u32[]{:S(2)}) collective-permute-start(bf16[64,2048]{1,0:T(8,128)(2,1)} %collective-permute-done.14.refs_2_), channel_id=1, source_target_pairs={{0,4},{4,8},{8,12},{12,16},{16,20},{20,24},{24,28},{28,0},{1,5},{5... | collective-permute-start | bytes 786440 | tf_op jit(solution)/shard_map/ppermute | solution.py:34
  78.4 13.8 %collective-permute-start.2 = (bf16[128,1792]{1,0:T(8,128)(2,1)}, bf16[128,1792]{1,0:T(8,128)(2,1)S(1)}, u32[]{:S(2)}, u32[]{:S(2)}) collective-permute-start(bf16[128,1792]{1,0:T(8,128)(2,1)} %get-tuple-element.43), channel_id=1, source_target_pairs={{0,128},{64,192},{128,0},{192,64},{1,129},{65,193},{129,1},{193,65... | collective-permute-start | bytes 1376264 | tf_op jit(solution)/shard_map/ppermute | solution.py:34
  83.6 8.6 %collective-permute-start.20 = (bf16[32,2048]{1,0:T(8,128)(2,1)}, bf16[32,2048]{1,0:T(8,128)(2,1)S(1)}, u32[]{:S(2)}, u32[]{:S(2)}) collective-permute-start(bf16[32,2048]{1,0:T(8,128)(2,1)} %slice.30), channel_id=1, source_target_pairs={{0,28},{4,0},{8,4},{12,8},{16,12},{20,16},{24,20},{28,24},{1,29},{... | collective-permute-start | bytes 393224 | tf_op jit(solution)/shard_map/ppermute | solution.py:34
  86.3 5.9 %collective-permute-start.16 = (bf16[32,2048]{1,0:T(8,128)(2,1)}, bf16[32,2048]{1,0:T(8,128)(2,1)}, u32[]{:S(2)}, u32[]{:S(2)}) collective-permute-start(bf16[32,2048]{1,0:T(8,128)(2,1)} %slice.29), channel_id=1, source_target_pairs={{0,4},{4,8},{8,12},{12,16},{16,20},{20,24},{24,28},{28,0},{1,5},{5... | collective-permute-start | bytes 393224 | tf_op jit(solution)/shard_map/ppermute | solution.py:34
  105.2 23.9 %all-to-all-start.2 = ((bf16[32,24,224]{2,1,0:T(8,128)(2,1)}), bf16[32,24,224]{2,1,0:T(8,128)(2,1)S(1)}, u32[]{:S(2)}, u32[]{:S(2)}) async-start(bf16[32,24,224]{2,1,0:T(8,128)(2,1)} %copy-done.7), calls=%async_computation.2 | async-start | bytes 786432 | tf_op jit(solution)/shard_map/all_to_all | solution.py:439
  129.4 8.9 %collective-permute-start.23 = (bf16[24,7168]{1,0:T(8,128)(2,1)S(1)}, bf16[24,7168]{1,0:T(8,128)(2,1)S(1)}, u32[]{:S(2)}, u32[]{:S(2)}) collective-permute-start(bf16[24,7168]{1,0:T(8,128)(2,1)S(1)} %norm.1.refs_0_), channel_id=1, source_target_pairs={{0,192},{64,0},{128,64},{192,128},{1,193},{65,1},{129,65},{193,129... | collective-permute-start | bytes 1032200 | tf_op jit(solution)/shard_map/ppermute | solution.py:34
  130.6 9.0 %collective-permute-start.21 = (bf16[24,7168]{1,0:T(8,128)(2,1)S(1)}, bf16[24,7168]{1,0:T(8,128)(2,1)S(1)}, u32[]{:S(2)}, u32[]{:S(2)}) collective-permute-start(bf16[24,7168]{1,0:T(8,128)(2,1)S(1)} %norm.1.refs_0_), channel_id=1, source_target_pairs={{0,64},{64,128},{128,192},{192,0},{1,65},{65,129},{129,193},{193,1... | collective-permute-start | bytes 1032200 | tf_op jit(solution)/shard_map/ppermute | solution.py:34
  131.5 14.9 %collective-permute-start.25 = (bf16[24,7168]{1,0:T(8,128)(2,1)S(1)}, bf16[24,7168]{1,0:T(8,128)(2,1)S(1)}, u32[]{:S(2)}, u32[]{:S(2)}) collective-permute-start(bf16[24,7168]{1,0:T(8,128)(2,1)S(1)} %norm.1.refs_0_), channel_id=1, source_target_pairs={{0,32},{32,0},{1,33},{33,1},{2,34},{34,2},{3,35},{35,3},{4,36},{36... | collective-permute-start | bytes 1032200 | tf_op jit(solution)/shard_map/ppermute | solution.py:34
  139.7 6.7 %collective-permute-start.22 = (bf16[24,3584]{1,0:T(8,128)(2,1)S(1)}, bf16[24,3584]{1,0:T(8,128)(2,1)S(1)}, u32[]{:S(2)}, u32[]{:S(2)}) collective-permute-start(bf16[24,3584]{1,0:T(8,128)(2,1)S(1)} %slice.31), channel_id=1, source_target_pairs={{0,64},{64,128},{128,192},{192,0},{1,65},{65,129},{129,193},{193,1... | collective-permute-start | bytes 516104 | tf_op jit(solution)/shard_map/ppermute | solution.py:34
  140.5 7.2 %collective-permute-start.26 = (bf16[24,7168]{1,0:T(8,128)(2,1)S(1)}, bf16[24,7168]{1,0:T(8,128)(2,1)S(1)}, u32[]{:S(2)}, u32[]{:S(2)}) collective-permute-start(bf16[24,7168]{1,0:T(8,128)(2,1)S(1)} %collective-permute-done.21.refs_1_), channel_id=1, source_target_pairs={{0,32},{32,0},{1,33},{33,1},{2,34},{34,2},{3,35},{35,3},{4,36},{36... | collective-permute-start | bytes 1032200 | tf_op jit(solution)/shard_map/ppermute | solution.py:34
  163.4 6.7 %collective-permute-start.35 = (bf16[24,1792]{1,0:T(8,128)(2,1)S(1)}, bf16[24,1792]{1,0:T(8,128)(2,1)S(1)}, u32[]{:S(2)}, u32[]{:S(2)}) collective-permute-start(bf16[24,1792]{1,0:T(8,128)(2,1)S(1)} %get-tuple-element.69), channel_id=1, source_target_pairs={{0,128},{64,192},{128,0},{192,64},{1,129},{65,193},{129,1},{193,65... | collective-permute-start | bytes 258056 | tf_op jit(solution)/shard_map/ppermute | solution.py:34
  164.3 6.7 %collective-permute-start.36 = (bf16[24,1792]{1,0:T(8,128)(2,1)S(1)}, bf16[24,1792]{1,0:T(8,128)(2,1)S(1)}, u32[]{:S(2)}, u32[]{:S(2)}) collective-permute-start(bf16[24,1792]{1,0:T(8,128)(2,1)S(1)} %get-tuple-element.70), channel_id=1, source_target_pairs={{0,64},{64,128},{128,192},{192,0},{1,65},{65,129},{129,193},{193,1... | collective-permute-start | bytes 258056 | tf_op jit(solution)/shard_map/ppermute | solution.py:34
  (32 other events, 315.7 us)

commit v3 on v2

--- a/solution.py
+++ b/solution.py
@@ -38,7 +38,7 @@
     return lax.ppermute(x, axis, [(i, i ^ mask) for i in range(lax.axis_size(axis))])
 
 
-def ring_gather(x, axis, dim):
+def ring_gather(x, axis, dim, beside=None):
     n = lax.axis_size(axis)
     far = n // 2
     cut = x.shape[dim] // 2
@@ -46,11 +46,14 @@
     right, left = x, x
     for step in range(1, far):
         right, left = shifted(right, axis, 1), shifted(left, axis, -1)
+        if step == 2:
+            left, beside = lax.optimization_barrier((left, beside))
         found[step], found[n - step] = right, left
     low = lax.slice_in_dim(right, 0, cut, axis=dim)
     high = lax.slice_in_dim(left, cut, x.shape[dim], axis=dim)
     found[far] = (shifted(low, axis, 1), shifted(high, axis, -1))
-    return [found[d] for d in range(n)]
+    pieces = [found[d] for d in range(n)]
+    return pieces if beside is None else (pieces, beside)
 
 
 def flat(pieces):
@@ -504,11 +507,12 @@
     (attention,) = new_attention(lens, at, queries, value_up, resident, pieces, 1)
 
     along_y = [attention] + [across(attention, COLUMN, d) for d in range(1, n_y)]
-    rows_here = flat(ring_gather(stacked(along_y), EXPERT[0], 0))
-    downs[2] = shifted(downs[2], HEAD[0], 2)
     block = lambda a: lax.dynamic_slice_in_dim(a, head * block_rows, block_rows)
     planned = plan(block(expert_ids), block(expert_gates), rows_dev, n_expert)
-    downs, rows_here, (sel, mix), kept = lax.optimization_barrier((downs, rows_here, planned, block(residual)))
+    rows_here, ((sel, mix), kept) = ring_gather(stacked(along_y), EXPERT[0], 0, (planned, block(residual)))
+    rows_here = flat(rows_here)
+    downs[2] = shifted(downs[2], HEAD[0], 2)
+    downs, rows_here = lax.optimization_barrier((downs, rows_here))
     away = jnp.arange(n_expert, dtype=I32)
     maker_z = (z + n_z - away // n_y) % n_z
     maker_y = y ^ (away % n_y)

time: 194 us -> 195 us (level)
  local copies, waits for them, and re-layouts: 15.2 us -> 11 us
  waiting for transfers between devices: 73.6 us -> 77.2 us
    ppermute x34, waiting for transfers between devices: 53.3 us -> 56.9 us  [shifted(): return lax.ppermute(x, axis, [(i, (i + step) % n) for i in range(n)])]
    unnamed x36, local copies, waits for them, and re-layouts: 8.75 us -> 6 us
  transfers between devices with their start and end apart: 39 -> 39, of which waited for: 25 -> 27; matrix products, arithmetic and copies ran while one was open for 7% -> 6% of each run, Pallas kernels for 0% -> 0%
where the time goes in v3:
time: 195 us; the launch traced here: 194 us
  waiting for transfers between devices  77.2 us (40%)
  starting transfers between devices  52 us (27%)
  blocking collectives  31.3 us (16%)
  Pallas kernels  16.4 us (8%)
  local copies, waits for them, and re-layouts  11 us (6%)
  matrix products  5.07 us (3%)
    ppermute x34, waiting for transfers between devices, shifted(): return lax.ppermute(x, axis, [(i, (i + step) % n) for i in range(n)])  56.9 us
    all_to_all x2, blocking collectives, exchange(): return lax.all_to_all(x, axes, split_axis=0, concat_axis=0, tiled=True)  31.3 us
    ppermute x34, starting transfers between devices, shifted(): return lax.ppermute(x, axis, [(i, (i + step) % n) for i in range(n)])  26.7 us
    all_to_all x2, starting transfers between devices, exchange(): return lax.all_to_all(x, axes, split_axis=0, concat_axis=0, tiled=True)  21.2 us
    all_to_all x2, waiting for transfers between devices, exchange(): return lax.all_to_all(x, axes, split_axis=0, concat_axis=0, tiled=True)  16.4 us
    unnamed x36, local copies, waits for them, and re-layouts  6 us
    pallas_call x1, Pallas kernels, new_attention(): pl.pallas_call(functools.partial(new_attention_kernel, groups), out_shape...  5.54 us
    ppermute x3, starting transfers between devices, across(): lax.ppermute(x, axis, [(i, i ^ mask) for i in range(lax.axis_size(axis))])  4.18 us
  transfers between devices with their start and end apart: 39, of which 27 were waited for; matrix products, arithmetic and copies ran while one was open for 6% of the time, Pallas kernels for 0%

profile of v3, /device:TPU:32, one launch (start us, length us, event | category | flops | bytes accessed | tf_op | source)
XLA Modules:
  0.0 194.1 jit_solution(17434148569559652137)
XLA Ops:
  3.3 11.4 %all-to-all-start = ((bf16[32,16,576]{2,1,0:T(8,128)(2,1)}), bf16[32,16,576]{2,1,0:T(8,128)(2,1)S(1)}, u32[]{:S(2)}, u32[]{:S(2)}) async-start(bf16[32,16,576]{2,1,0:T(8,128)(2,1)} %pack_cache.1), calls=%async_computation | async-start | bytes 1310720 | tf_op jit(solution)/shard_map/all_to_all | solution.py:442
  15.9 2.8 %collective-permute-start.1 = (bf16[128,1792]{1,0:T(8,128)(2,1)}, bf16[128,1792]{1,0:T(8,128)(2,1)}, u32[]{:S(2)}, u32[]{:S(2)}) collective-permute-start(bf16[128,1792]{1,0:T(8,128)(2,1)} %get-tuple-element.77), channel_id=1, source_target_pairs={{0,192},{64,0},{128,64},{192,128},{1,193},{65,1},{129,65},{193,129... | collective-permute-start | bytes 1376264 | tf_op jit(solution)/shard_map/ppermute | solution.py:34
  21.0 2.3 %fusion.4 = bf16[4,16,512]{2,1,0:T(8,128)(2,1)} fusion(bf16[4,576,256]{2,1,0:T(8,128)(2,1)} %bitcast.19, f32[4,16]{1,0:T(4,128)S(1)} %fusion.18, f32[4,16,256]{2,1,0:T(8,128)S(1)} %fusion.2), kind=kOutput, calls=%fused_computation.6 | convolution fusion | flops 16826688 | bytes 1247232 | tf_op jit(solution)/shard_map/rht,rct->rhc/dot_general | solution.py:75
  24.4 3.8 %collective-permute-done.1.refs_7_ = bf16[128,1792]{1,0:T(8,128)(2,1)} collective-permute-done((bf16[128,1792]{1,0:T(8,128)(2,1)}, bf16[128,1792]{1,0:T(8,128)(2,1)}, u32[]{:S(2)}, u32[]{:S(2)}) %collective-permute-start.1) | collective-permute-done | bytes 458784 | tf_op jit(solution)/shard_map/ppermute | solution.py:34
  28.2 3.4 %collective-permute-done.refs_5_ = bf16[128,1792]{1,0:T(8,128)(2,1)} collective-permute-done((bf16[128,1792]{1,0:T(8,128)(2,1)}, bf16[128,1792]{1,0:T(8,128)(2,1)}, u32[]{:S(2)}, u32[]{:S(2)}) %collective-permute-start) | collective-permute-done | bytes 458784 | tf_op jit(solution)/shard_map/ppermute | solution.py:34
  31.6 2.8 %all-to-all-done.arrived_ref = bf16[32,16,576]{2,1,0:T(8,128)(2,1)S(1)} async-done(((bf16[32,16,576]{2,1,0:T(8,128)(2,1)}), bf16[32,16,576]{2,1,0:T(8,128)(2,1)S(1)}, u32[]{:S(2)}, u32[]{:S(2)}) %all-to-all-start) | async-done | bytes 589856 | tf_op jit(solution)/shard_map/all_to_all | solution.py:442
  35.7 2.8 %collective-permute-start.5 = (bf16[6,16,576]{2,1,0:T(8,128)(2,1)}, bf16[6,16,576]{2,1,0:T(8,128)(2,1)S(1)}, u32[]{:S(2)}, u32[]{:S(2)}) collective-permute-start(bf16[6,16,576]{2,1,0:T(8,128)(2,1)} %select_arrived.1.refs_0_), channel_id=1, source_target_pairs={{0,192},{64,0},{128,64},{192,128},{1,193},{65,1},{129,65},{193,129... | collective-permute-start | bytes 331784 | tf_op jit(solution)/shard_map/ppermute | solution.py:34
  41.3 3.9 %collective-permute-done.4.refs_2_ = bf16[6,16,576]{2,1,0:T(8,128)(2,1)S(1)} collective-permute-done((bf16[6,16,576]{2,1,0:T(8,128)(2,1)}, bf16[6,16,576]{2,1,0:T(8,128)(2,1)S(1)}, u32[]{:S(2)}, u32[]{:S(2)}) %collective-permute-start.4) | collective-permute-done | bytes 110624 | tf_op jit(solution)/shard_map/ppermute | solution.py:34
  48.8 5.5 %new_attention.1.refs_0_ = bf16[16,2048]{1,0:T(8,128)(2,1)S(1)} custom-call(s32[12]{0:T(128)S(1)} %get-tuple-element.76.lens, s32[3]{0:T(128)S(1)} %pad_add_fusion.at, bf16[16,16,576]{2,1,0:T(8,128)(2,1)S(1)} %copy-done.5, bf16[16,512,128]{2,1,0:T(8,128)(2,1)S(1)} %copy-done.1, bf16[16,4,128]{2,1,0:T(4,128)(2,1)S(1)} %convolution_convert_fusion.res_ref, ...), custom_call_target="tpu_custom_call" | custom-call | tf_op jit(solution)/shard_map/new_attention/pallas_call | solution.py:184
  59.9 2.5 %collective-permute-done.11.refs_2_ = bf16[16,2048]{1,0:T(8,128)(2,1)S(1)} collective-permute-done((bf16[16,2048]{1,0:T(8,128)(2,1)S(1)}, bf16[16,2048]{1,0:T(8,128)(2,1)S(1)}, u32[]{:S(2)}, u32[]{:S(2)}) %collective-permute-start.11) | collective-permute-done | bytes 65568 | tf_op jit(solution)/shard_map/ppermute | solution.py:38
  64.6 4.6 %collective-permute-done.17.refs_8_ = bf16[64,2048]{1,0:T(8,128)(2,1)S(1)} collective-permute-done((bf16[64,2048]{1,0:T(8,128)(2,1)S(1)}, bf16[64,2048]{1,0:T(8,128)(2,1)S(1)}, u32[]{:S(2)}, u32[]{:S(2)}) %collective-permute-start.17) | collective-permute-done | bytes 262176 | tf_op jit(solution)/shard_map/ppermute | solution.py:34
  78.4 4.3 %collective-permute-done.19.refs_6_ = bf16[64,2048]{1,0:T(8,128)(2,1)S(1)} collective-permute-done((bf16[64,2048]{1,0:T(8,128)(2,1)}, bf16[64,2048]{1,0:T(8,128)(2,1)S(1)}, u32[]{:S(2)}, u32[]{:S(2)}) %collective-permute-start.19) | collective-permute-done | bytes 262176 | tf_op jit(solution)/shard_map/ppermute | solution.py:34
  83.3 2.3 %collective-permute-start.20 = (bf16[32,2048]{1,0:T(8,128)(2,1)}, bf16[32,2048]{1,0:T(8,128)(2,1)S(1)}, u32[]{:S(2)}, u32[]{:S(2)}) collective-permute-start(bf16[32,2048]{1,0:T(8,128)(2,1)} %slice.30), channel_id=1, source_target_pairs={{0,28},{4,0},{8,4},{12,8},{16,12},{20,16},{24,20},{28,24},{1,29},{... | collective-permute-start | bytes 393224 | tf_op jit(solution)/shard_map/ppermute | solution.py:34
  88.5 3.4 %collective-permute-done.16.refs_4_ = bf16[32,2048]{1,0:T(8,128)(2,1)} collective-permute-done((bf16[32,2048]{1,0:T(8,128)(2,1)}, bf16[32,2048]{1,0:T(8,128)(2,1)}, u32[]{:S(2)}, u32[]{:S(2)}) %collective-permute-start.16) | collective-permute-done | bytes 131104 | tf_op jit(solution)/shard_map/ppermute | solution.py:34
  93.8 11.0 %all_to_all.20.parts_ref = bf16[8,64,224]{2,1,0:T(8,128)(2,1)S(1)} all-to-all(bf16[8,64,224]{2,1,0:T(8,128)(2,1)S(1)} %bitcast.16), channel_id=1, replica_groups=mesh['head_0'=4,'head_1'=2,'expert_0'=8,'expert_1'=2,'expert_2'=2] {'hea..., dimensions={0} | all-to-all | bytes 458752 | tf_op jit(solution)/shard_map/all_to_all | solution.py:442
  105.9 9.8 %all-to-all-start.2 = ((bf16[32,24,224]{2,1,0:T(8,128)(2,1)}), bf16[32,24,224]{2,1,0:T(8,128)(2,1)S(1)}, u32[]{:S(2)}, u32[]{:S(2)}) async-start(bf16[32,24,224]{2,1,0:T(8,128)(2,1)} %copy-done.7), calls=%async_computation.2 | async-start | bytes 786432 | tf_op jit(solution)/shard_map/all_to_all | solution.py:442
  116.4 13.6 %all-to-all-done.2.x_ref = bf16[32,24,224]{2,1,0:T(8,128)(2,1)S(1)} async-done(((bf16[32,24,224]{2,1,0:T(8,128)(2,1)}), bf16[32,24,224]{2,1,0:T(8,128)(2,1)S(1)}, u32[]{:S(2)}, u32[]{:S(2)}) %all-to-all-start.2) | async-done | bytes 344096 | tf_op jit(solution)/shard_map/all_to_all | solution.py:442
  132.3 6.8 %collective-permute-done.23.refs_4_ = bf16[24,7168]{1,0:T(8,128)(2,1)S(1)} collective-permute-done((bf16[24,7168]{1,0:T(8,128)(2,1)S(1)}, bf16[24,7168]{1,0:T(8,128)(2,1)S(1)}, u32[]{:S(2)}, u32[]{:S(2)}) %collective-permute-start.23) | collective-permute-done | bytes 344096 | tf_op jit(solution)/shard_map/ppermute | solution.py:34
  141.9 2.8 %collective-permute-done.24.refs_3_ = bf16[24,3584]{1,0:T(8,128)(2,1)S(1)} collective-permute-done((bf16[24,3584]{1,0:T(8,128)(2,1)S(1)}, bf16[24,3584]{1,0:T(8,128)(2,1)S(1)}, u32[]{:S(2)}, u32[]{:S(2)}) %collective-permute-start.24) | collective-permute-done | bytes 172064 | tf_op jit(solution)/shard_map/ppermute | solution.py:34
  144.7 2.6 %collective-permute-done.22.refs_2_ = bf16[24,3584]{1,0:T(8,128)(2,1)S(1)} collective-permute-done((bf16[24,3584]{1,0:T(8,128)(2,1)S(1)}, bf16[24,3584]{1,0:T(8,128)(2,1)S(1)}, u32[]{:S(2)}, u32[]{:S(2)}) %collective-permute-start.22) | collective-permute-done | bytes 172064 | tf_op jit(solution)/shard_map/ppermute | solution.py:34
  153.8 2.3 %collective-permute-done.32.refs_3_ = bf16[192,128]{1,0:T(8,128)(2,1)S(1)} collective-permute-done((bf16[192,128]{1,0:T(8,128)(2,1)S(1)}, bf16[192,128]{1,0:T(8,128)(2,1)S(1)}, u32[]{:S(2)}, u32[]{:S(2)}) %collective-permute-start.32) | collective-permute-done | bytes 49184 | tf_op jit(solution)/shard_map/ppermute | solution.py:34
  165.2 3.0 %collective-permute-done.34.refs_1_ = bf16[24,1792]{1,0:T(8,128)(2,1)S(1)} collective-permute-done((bf16[24,1792]{1,0:T(8,128)(2,1)S(1)}, bf16[24,1792]{1,0:T(8,128)(2,1)S(1)}, u32[]{:S(2)}, u32[]{:S(2)}) %collective-permute-start.34) | collective-permute-done | bytes 86048 | tf_op jit(solution)/shard_map/ppermute | solution.py:34
  168.2 2.8 %collective-permute-done.35.refs_2_ = bf16[24,1792]{1,0:T(8,128)(2,1)S(1)} collective-permute-done((bf16[24,1792]{1,0:T(8,128)(2,1)S(1)}, bf16[24,1792]{1,0:T(8,128)(2,1)S(1)}, u32[]{:S(2)}, u32[]{:S(2)}) %collective-permute-start.35) | collective-permute-done | bytes 86048 | tf_op jit(solution)/shard_map/ppermute | solution.py:34
  172.6 20.3 %all_to_all.21.back_ref = bf16[32,24,224]{2,1,0:T(8,128)(2,1)S(1)} all-to-all(bf16[32,24,224]{2,1,0:T(8,128)(2,1)S(1)} %by_columns.1), channel_id=1, replica_groups=mesh['head_0'=4,'head_1'=2,'expert_0'=8,'expert_1'=2,'expert_2'=2] {'exp..., dimensions={0} | all-to-all | bytes 688128 | tf_op jit(solution)/shard_map/all_to_all | solution.py:442
  (126 shorter events, 63.0 us)
Async XLA Ops:
  3.3 31.2 %all-to-all-start = ((bf16[32,16,576]{2,1,0:T(8,128)(2,1)}), bf16[32,16,576]{2,1,0:T(8,128)(2,1)S(1)}, u32[]{:S(2)}, u32[]{:S(2)}) async-start(bf16[32,16,576]{2,1,0:T(8,128)(2,1)} %pack_cache.1), calls=%async_computation | async-start | bytes 1310720 | tf_op jit(solution)/shard_map/all_to_all | solution.py:442
  15.9 12.3 %collective-permute-start.1 = (bf16[128,1792]{1,0:T(8,128)(2,1)}, bf16[128,1792]{1,0:T(8,128)(2,1)}, u32[]{:S(2)}, u32[]{:S(2)}) collective-permute-start(bf16[128,1792]{1,0:T(8,128)(2,1)} %get-tuple-element.77), channel_id=1, source_target_pairs={{0,192},{64,0},{128,64},{192,128},{1,193},{65,1},{129,65},{193,129... | collective-permute-start | bytes 1376264 | tf_op jit(solution)/shard_map/ppermute | solution.py:34
  18.7 13.0 %collective-permute-start = (bf16[128,1792]{1,0:T(8,128)(2,1)}, bf16[128,1792]{1,0:T(8,128)(2,1)}, u32[]{:S(2)}, u32[]{:S(2)}) collective-permute-start(bf16[128,1792]{1,0:T(8,128)(2,1)} %get-tuple-element.79), channel_id=1, source_target_pairs={{0,64},{64,128},{128,192},{192,0},{1,65},{65,129},{129,193},{193,1... | collective-permute-start | bytes 1376264 | tf_op jit(solution)/shard_map/ppermute | solution.py:34
  38.6 6.7 %collective-permute-start.4 = (bf16[6,16,576]{2,1,0:T(8,128)(2,1)}, bf16[6,16,576]{2,1,0:T(8,128)(2,1)S(1)}, u32[]{:S(2)}, u32[]{:S(2)}) collective-permute-start(bf16[6,16,576]{2,1,0:T(8,128)(2,1)} %select_arrived.1.refs_0_), channel_id=1, source_target_pairs={{0,128},{64,192},{128,0},{192,64},{1,129},{65,193},{129,1},{193,65... | collective-permute-start | bytes 331784 | tf_op jit(solution)/shard_map/ppermute | solution.py:34
  39.4 7.1 %collective-permute-start.3 = (bf16[6,16,576]{2,1,0:T(8,128)(2,1)}, bf16[6,16,576]{2,1,0:T(8,128)(2,1)S(1)}, u32[]{:S(2)}, u32[]{:S(2)}) collective-permute-start(bf16[6,16,576]{2,1,0:T(8,128)(2,1)} %select_arrived.1.refs_0_), channel_id=1, source_target_pairs={{0,64},{64,128},{128,192},{192,0},{1,65},{65,129},{129,193},{193,1... | collective-permute-start | bytes 331784 | tf_op jit(solution)/shard_map/ppermute | solution.py:34
  40.3 6.3 %collective-permute-start.6 = (bf16[6,16,576]{2,1,0:T(8,128)(2,1)}, bf16[6,16,576]{2,1,0:T(8,128)(2,1)S(1)}, u32[]{:S(2)}, u32[]{:S(2)}) collective-permute-start(bf16[6,16,576]{2,1,0:T(8,128)(2,1)} %select_arrived.1.refs_0_), channel_id=1, source_target_pairs={{0,32},{32,0},{1,33},{33,1},{2,34},{34,2},{3,35},{35,3},{4,36},{36... | collective-permute-start | bytes 331784 | tf_op jit(solution)/shard_map/ppermute | solution.py:34
  56.4 6.1 %collective-permute-start.11 = (bf16[16,2048]{1,0:T(8,128)(2,1)S(1)}, bf16[16,2048]{1,0:T(8,128)(2,1)S(1)}, u32[]{:S(2)}, u32[]{:S(2)}) collective-permute-start(bf16[16,2048]{1,0:T(8,128)(2,1)S(1)} %new_attention.1.refs_0_), channel_id=1, source_target_pairs={{0,2},{1,3},{2,0},{3,1},{4,6},{5,7},{6,4},{7,5},{8,10},{9,11},{10,... | collective-permute-start | bytes 196616 | tf_op jit(solution)/shard_map/ppermute | solution.py:38
  62.5 6.7 %collective-permute-start.17 = (bf16[64,2048]{1,0:T(8,128)(2,1)S(1)}, bf16[64,2048]{1,0:T(8,128)(2,1)S(1)}, u32[]{:S(2)}, u32[]{:S(2)}) collective-permute-start(bf16[64,2048]{1,0:T(8,128)(2,1)S(1)} %stack.17.refs_0_), channel_id=1, source_target_pairs={{0,28},{4,0},{8,4},{12,8},{16,12},{20,16},{24,20},{28,24},{1,29},{... | collective-permute-start | bytes 786440 | tf_op jit(solution)/shard_map/ppermute | solution.py:34
  63.7 6.6 %collective-permute-start.13 = (bf16[64,2048]{1,0:T(8,128)(2,1)S(1)}, bf16[64,2048]{1,0:T(8,128)(2,1)S(1)}, u32[]{:S(2)}, u32[]{:S(2)}) collective-permute-start(bf16[64,2048]{1,0:T(8,128)(2,1)S(1)} %stack.17.refs_0_), channel_id=1, source_target_pairs={{0,4},{4,8},{8,12},{12,16},{16,20},{20,24},{24,28},{28,0},{1,5},{5... | collective-permute-start | bytes 786440 | tf_op jit(solution)/shard_map/ppermute | solution.py:34
  69.2 6.9 %collective-permute-start.18 = (bf16[64,2048]{1,0:T(8,128)(2,1)S(1)}, bf16[64,2048]{1,0:T(8,128)(2,1)}, u32[]{:S(2)}, u32[]{:S(2)}) collective-permute-start(bf16[64,2048]{1,0:T(8,128)(2,1)S(1)} %collective-permute-done.17.refs_8_), channel_id=1, source_target_pairs={{0,28},{4,0},{8,4},{12,8},{16,12},{20,16},{24,20},{28,24},{1,29},{... | collective-permute-start | bytes 786440 | tf_op jit(solution)/shard_map/ppermute | solution.py:34
  70.3 7.2 %collective-permute-start.14 = (bf16[64,2048]{1,0:T(8,128)(2,1)S(1)}, bf16[64,2048]{1,0:T(8,128)(2,1)}, u32[]{:S(2)}, u32[]{:S(2)}) collective-permute-start(bf16[64,2048]{1,0:T(8,128)(2,1)S(1)} %collective-permute-done.13.refs_1_), channel_id=1, source_target_pairs={{0,4},{4,8},{8,12},{12,16},{16,20},{20,24},{24,28},{28,0},{1,5},{5... | collective-permute-start | bytes 786440 | tf_op jit(solution)/shard_map/ppermute | solution.py:34
  72.9 13.4 %collective-permute-start.2 = (bf16[128,1792]{1,0:T(8,128)(2,1)}, bf16[128,1792]{1,0:T(8,128)(2,1)S(1)}, u32[]{:S(2)}, u32[]{:S(2)}) collective-permute-start(bf16[128,1792]{1,0:T(8,128)(2,1)} %get-tuple-element.44), channel_id=1, source_target_pairs={{0,128},{64,192},{128,0},{192,64},{1,129},{65,193},{129,1},{193,65... | collective-permute-start | bytes 1376264 | tf_op jit(solution)/shard_map/ppermute | solution.py:34
  76.1 6.6 %collective-permute-start.19 = (bf16[64,2048]{1,0:T(8,128)(2,1)}, bf16[64,2048]{1,0:T(8,128)(2,1)S(1)}, u32[]{:S(2)}, u32[]{:S(2)}) collective-permute-start(bf16[64,2048]{1,0:T(8,128)(2,1)} %collective-permute-done.18.refs_7_), channel_id=1, source_target_pairs={{0,28},{4,0},{8,4},{12,8},{16,12},{20,16},{24,20},{28,24},{1,29},{... | collective-permute-start | bytes 786440 | tf_op jit(solution)/shard_map/ppermute | solution.py:34
  77.5 8.1 %collective-permute-start.15 = (bf16[64,2048]{1,0:T(8,128)(2,1)}, bf16[64,2048]{1,0:T(8,128)(2,1)S(1)}, u32[]{:S(2)}, u32[]{:S(2)}) collective-permute-start(bf16[64,2048]{1,0:T(8,128)(2,1)} %collective-permute-done.14.refs_2_), channel_id=1, source_target_pairs={{0,4},{4,8},{8,12},{12,16},{16,20},{20,24},{24,28},{28,0},{1,5},{5... | collective-permute-start | bytes 786440 | tf_op jit(solution)/shard_map/ppermute | solution.py:34
  105.9 24.2 %all-to-all-start.2 = ((bf16[32,24,224]{2,1,0:T(8,128)(2,1)}), bf16[32,24,224]{2,1,0:T(8,128)(2,1)S(1)}, u32[]{:S(2)}, u32[]{:S(2)}) async-start(bf16[32,24,224]{2,1,0:T(8,128)(2,1)} %copy-done.7), calls=%async_computation.2 | async-start | bytes 786432 | tf_op jit(solution)/shard_map/all_to_all | solution.py:442
  130.2 8.9 %collective-permute-start.23 = (bf16[24,7168]{1,0:T(8,128)(2,1)S(1)}, bf16[24,7168]{1,0:T(8,128)(2,1)S(1)}, u32[]{:S(2)}, u32[]{:S(2)}) collective-permute-start(bf16[24,7168]{1,0:T(8,128)(2,1)S(1)} %norm.1.refs_0_), channel_id=1, source_target_pairs={{0,192},{64,0},{128,64},{192,128},{1,193},{65,1},{129,65},{193,129... | collective-permute-start | bytes 1032200 | tf_op jit(solution)/shard_map/ppermute | solution.py:34
  131.5 9.0 %collective-permute-start.21 = (bf16[24,7168]{1,0:T(8,128)(2,1)S(1)}, bf16[24,7168]{1,0:T(8,128)(2,1)S(1)}, u32[]{:S(2)}, u32[]{:S(2)}) collective-permute-start(bf16[24,7168]{1,0:T(8,128)(2,1)S(1)} %norm.1.refs_0_), channel_id=1, source_target_pairs={{0,64},{64,128},{128,192},{192,0},{1,65},{65,129},{129,193},{193,1... | collective-permute-start | bytes 1032200 | tf_op jit(solution)/shard_map/ppermute | solution.py:34
  132.3 14.9 %collective-permute-start.25 = (bf16[24,7168]{1,0:T(8,128)(2,1)S(1)}, bf16[24,7168]{1,0:T(8,128)(2,1)S(1)}, u32[]{:S(2)}, u32[]{:S(2)}) collective-permute-start(bf16[24,7168]{1,0:T(8,128)(2,1)S(1)} %norm.1.refs_0_), channel_id=1, source_target_pairs={{0,32},{32,0},{1,33},{33,1},{2,34},{34,2},{3,35},{35,3},{4,36},{36... | collective-permute-start | bytes 1032200 | tf_op jit(solution)/shard_map/ppermute | solution.py:34
  140.5 6.7 %collective-permute-start.22 = (bf16[24,3584]{1,0:T(8,128)(2,1)S(1)}, bf16[24,3584]{1,0:T(8,128)(2,1)S(1)}, u32[]{:S(2)}, u32[]{:S(2)}) collective-permute-start(bf16[24,3584]{1,0:T(8,128)(2,1)S(1)} %slice.31), channel_id=1, source_target_pairs={{0,64},{64,128},{128,192},{192,0},{1,65},{65,129},{129,193},{193,1... | collective-permute-start | bytes 516104 | tf_op jit(solution)/shard_map/ppermute | solution.py:34
  141.4 5.9 %collective-permute-start.29 = (bf16[24,7168]{1,0:T(8,128)(2,1)S(1)}, bf16[24,7168]{1,0:T(8,128)(2,1)S(1)}, u32[]{:S(2)}, u32[]{:S(2)}) collective-permute-start(bf16[24,7168]{1,0:T(8,128)(2,1)S(1)} %collective-permute-done.23.refs_4_), channel_id=1, source_target_pairs={{0,32},{32,0},{1,33},{33,1},{2,34},{34,2},{3,35},{35,3},{4,36},{36... | collective-permute-start | bytes 1032200 | tf_op jit(solution)/shard_map/ppermute | solution.py:34
  141.4 7.3 %collective-permute-start.26 = (bf16[24,7168]{1,0:T(8,128)(2,1)S(1)}, bf16[24,7168]{1,0:T(8,128)(2,1)S(1)}, u32[]{:S(2)}, u32[]{:S(2)}) collective-permute-start(bf16[24,7168]{1,0:T(8,128)(2,1)S(1)} %collective-permute-done.21.refs_1_), channel_id=1, source_target_pairs={{0,32},{32,0},{1,33},{33,1},{2,34},{34,2},{3,35},{35,3},{4,36},{36... | collective-permute-start | bytes 1032200 | tf_op jit(solution)/shard_map/ppermute | solution.py:34
  162.3 5.9 %collective-permute-start.34 = (bf16[24,1792]{1,0:T(8,128)(2,1)S(1)}, bf16[24,1792]{1,0:T(8,128)(2,1)S(1)}, u32[]{:S(2)}, u32[]{:S(2)}) collective-permute-start(bf16[24,1792]{1,0:T(8,128)(2,1)S(1)} %get-tuple-element.70), channel_id=1, source_target_pairs={{0,192},{64,0},{128,64},{192,128},{1,193},{65,1},{129,65},{193,129... | collective-permute-start | bytes 258056 | tf_op jit(solution)/shard_map/ppermute | solution.py:34
  164.2 6.7 %collective-permute-start.35 = (bf16[24,1792]{1,0:T(8,128)(2,1)S(1)}, bf16[24,1792]{1,0:T(8,128)(2,1)S(1)}, u32[]{:S(2)}, u32[]{:S(2)}) collective-permute-start(bf16[24,1792]{1,0:T(8,128)(2,1)S(1)} %get-tuple-element.71), channel_id=1, source_target_pairs={{0,128},{64,192},{128,0},{192,64},{1,129},{65,193},{129,1},{193,65... | collective-permute-start | bytes 258056 | tf_op jit(solution)/shard_map/ppermute | solution.py:34
  165.1 6.7 %collective-permute-start.36 = (bf16[24,1792]{1,0:T(8,128)(2,1)S(1)}, bf16[24,1792]{1,0:T(8,128)(2,1)S(1)}, u32[]{:S(2)}, u32[]{:S(2)}) collective-permute-start(bf16[24,1792]{1,0:T(8,128)(2,1)S(1)} %get-tuple-element.72), channel_id=1, source_target_pairs={{0,64},{64,128},{128,192},{192,0},{1,65},{65,129},{129,193},{193,1... | collective-permute-start | bytes 258056 | tf_op jit(solution)/shard_map/ppermute | solution.py:34
  (32 other events, 331.2 us)

commit v4 on v3

--- a/solution.py
+++ b/solution.py
@@ -154,20 +154,24 @@
     place, core, row = at[0], at[1], at[2]
     column = lax.broadcasted_iota(I32, (heads, ring * span), 1)
     position = ((place + ring - column // span) % ring) * span + column % span
+
+    def cache(i):
+        k, ours = i // MOST, core == i % MOST
+        return jnp.concatenate([jnp.where(ours, pieces[d][k], pieces[ring + d][k]) for d in range(ring)], axis=0)
+
+    rows = []
     for i in range(count):
-        k, turn = i // MOST, i % MOST
-        ours = core == turn
-        cache = jnp.concatenate(
-            [jnp.where(ours, pieces[d][k], pieces[ring + d][k]) for d in range(ring)], axis=0
+        scores = lax.dot_general(
+            q_ref[old + i], cache(i), (((1,), (1,)), ((), ())), preferred_element_type=F32
         )
-        scores = (
-            lax.dot_general(q_ref[old + i], cache, (((1,), (1,)), ((), ())), preferred_element_type=F32)
-            * inverse_root
+        rows.append(jnp.where(position < lens[i], scores * inverse_root, -jnp.inf))
+    scores = jnp.concatenate(rows, axis=0)
+    raised = jnp.exp(scores - jnp.max(scores, axis=1, keepdims=True))
+    weights = (raised / jnp.sum(raised, axis=1, keepdims=True)).astype(BF)
+    for i in range(count):
+        latents[:, i, :] = jnp.dot(
+            weights[i * heads : (i + 1) * heads], cache(i)[:, :latent_width], preferred_element_type=F32
         )
-        scores = jnp.where(position < lens[i], scores, -jnp.inf)
-        raised = jnp.exp(scores - jnp.max(scores, axis=1, keepdims=True))
-        weights = (raised / jnp.sum(raised, axis=1, keepdims=True)).astype(BF)
-        latents[:, i, :] = jnp.dot(weights, cache[:, :latent_width], preferred_element_type=F32)
     each = heads // groups
     for d, out_ref in enumerate(out_refs):
         for k in range(each):

time: 195 us -> 191 us (0.979)
  Pallas kernels: 16.4 us -> 12.9 us
    pallas_call x1, Pallas kernels: 5.54 us -> 2.05 us  [new_attention(): pl.pallas_call(functools.partial(new_attention_kernel, groups), out_shape...]
where the time goes in v4:
time: 191 us
  waiting for transfers between devices  77.2 us (40%)
  starting transfers between devices  52.1 us (27%)
  blocking collectives  31.3 us (16%)
  Pallas kernels  12.9 us (7%)
  local copies, waits for them, and re-layouts  11 us (6%)
  matrix products  5.07 us (3%)
    ppermute x34, waiting for transfers between devices, shifted(): return lax.ppermute(x, axis, [(i, (i + step) % n) for i in range(n)])  56.8 us
    all_to_all x2, blocking collectives, exchange(): return lax.all_to_all(x, axes, split_axis=0, concat_axis=0, tiled=True)  31.3 us
    ppermute x34, starting transfers between devices, shifted(): return lax.ppermute(x, axis, [(i, (i + step) % n) for i in range(n)])  26.8 us
    all_to_all x2, starting transfers between devices, exchange(): return lax.all_to_all(x, axes, split_axis=0, concat_axis=0, tiled=True)  21.2 us
    all_to_all x2, waiting for transfers between devices, exchange(): return lax.all_to_all(x, axes, split_axis=0, concat_axis=0, tiled=True)  16.4 us
    unnamed x36, local copies, waits for them, and re-layouts  6 us
    ppermute x3, starting transfers between devices, across(): lax.ppermute(x, axis, [(i, i ^ mask) for i in range(lax.axis_size(axis))])  4.18 us
    ppermute x3, waiting for transfers between devices, across(): lax.ppermute(x, axis, [(i, i ^ mask) for i in range(lax.axis_size(axis))])  3.91 us
  transfers between devices with their start and end apart: 39, of which 27 were waited for; matrix products, arithmetic and copies ran while one was open for 6% of the time, Pallas kernels for 0%

profile of v4, /device:TPU:32, one launch (start us, length us, event | category | flops | bytes accessed | tf_op | source)
XLA Modules:
  0.0 190.6 jit_solution(8066656303800879245)
XLA Ops:
  3.3 11.4 %all-to-all-start = ((bf16[32,16,576]{2,1,0:T(8,128)(2,1)}), bf16[32,16,576]{2,1,0:T(8,128)(2,1)S(1)}, u32[]{:S(2)}, u32[]{:S(2)}) async-start(bf16[32,16,576]{2,1,0:T(8,128)(2,1)} %pack_cache.1), calls=%async_computation | async-start | bytes 1310720 | tf_op jit(solution)/shard_map/all_to_all | solution.py:446
  15.9 2.8 %collective-permute-start.1 = (bf16[128,1792]{1,0:T(8,128)(2,1)}, bf16[128,1792]{1,0:T(8,128)(2,1)}, u32[]{:S(2)}, u32[]{:S(2)}) collective-permute-start(bf16[128,1792]{1,0:T(8,128)(2,1)} %get-tuple-element.77), channel_id=1, source_target_pairs={{0,192},{64,0},{128,64},{192,128},{1,193},{65,1},{129,65},{193,129... | collective-permute-start | bytes 1376264 | tf_op jit(solution)/shard_map/ppermute | solution.py:34
  21.0 2.3 %fusion.4 = bf16[4,16,512]{2,1,0:T(8,128)(2,1)} fusion(bf16[4,576,256]{2,1,0:T(8,128)(2,1)} %bitcast.19, f32[4,16]{1,0:T(4,128)S(1)} %fusion.18, f32[4,16,256]{2,1,0:T(8,128)S(1)} %fusion.2), kind=kOutput, calls=%fused_computation.6 | convolution fusion | flops 16826688 | bytes 1247232 | tf_op jit(solution)/shard_map/rht,rct->rhc/dot_general | solution.py:75
  24.5 3.8 %collective-permute-done.1.refs_7_ = bf16[128,1792]{1,0:T(8,128)(2,1)} collective-permute-done((bf16[128,1792]{1,0:T(8,128)(2,1)}, bf16[128,1792]{1,0:T(8,128)(2,1)}, u32[]{:S(2)}, u32[]{:S(2)}) %collective-permute-start.1) | collective-permute-done | bytes 458784 | tf_op jit(solution)/shard_map/ppermute | solution.py:34
  28.2 3.4 %collective-permute-done.refs_5_ = bf16[128,1792]{1,0:T(8,128)(2,1)} collective-permute-done((bf16[128,1792]{1,0:T(8,128)(2,1)}, bf16[128,1792]{1,0:T(8,128)(2,1)}, u32[]{:S(2)}, u32[]{:S(2)}) %collective-permute-start) | collective-permute-done | bytes 458784 | tf_op jit(solution)/shard_map/ppermute | solution.py:34
  31.7 2.8 %all-to-all-done.arrived_ref = bf16[32,16,576]{2,1,0:T(8,128)(2,1)S(1)} async-done(((bf16[32,16,576]{2,1,0:T(8,128)(2,1)}), bf16[32,16,576]{2,1,0:T(8,128)(2,1)S(1)}, u32[]{:S(2)}, u32[]{:S(2)}) %all-to-all-start) | async-done | bytes 589856 | tf_op jit(solution)/shard_map/all_to_all | solution.py:446
  35.7 2.8 %collective-permute-start.5 = (bf16[6,16,576]{2,1,0:T(8,128)(2,1)}, bf16[6,16,576]{2,1,0:T(8,128)(2,1)S(1)}, u32[]{:S(2)}, u32[]{:S(2)}) collective-permute-start(bf16[6,16,576]{2,1,0:T(8,128)(2,1)} %select_arrived.1.refs_0_), channel_id=1, source_target_pairs={{0,192},{64,0},{128,64},{192,128},{1,193},{65,1},{129,65},{193,129... | collective-permute-start | bytes 331784 | tf_op jit(solution)/shard_map/ppermute | solution.py:34
  41.3 3.9 %collective-permute-done.4.refs_2_ = bf16[6,16,576]{2,1,0:T(8,128)(2,1)S(1)} collective-permute-done((bf16[6,16,576]{2,1,0:T(8,128)(2,1)}, bf16[6,16,576]{2,1,0:T(8,128)(2,1)S(1)}, u32[]{:S(2)}, u32[]{:S(2)}) %collective-permute-start.4) | collective-permute-done | bytes 110624 | tf_op jit(solution)/shard_map/ppermute | solution.py:34
  56.4 2.5 %collective-permute-done.11.refs_2_ = bf16[16,2048]{1,0:T(8,128)(2,1)S(1)} collective-permute-done((bf16[16,2048]{1,0:T(8,128)(2,1)S(1)}, bf16[16,2048]{1,0:T(8,128)(2,1)S(1)}, u32[]{:S(2)}, u32[]{:S(2)}) %collective-permute-start.11) | collective-permute-done | bytes 65568 | tf_op jit(solution)/shard_map/ppermute | solution.py:38
  61.1 4.6 %collective-permute-done.17.refs_8_ = bf16[64,2048]{1,0:T(8,128)(2,1)S(1)} collective-permute-done((bf16[64,2048]{1,0:T(8,128)(2,1)S(1)}, bf16[64,2048]{1,0:T(8,128)(2,1)S(1)}, u32[]{:S(2)}, u32[]{:S(2)}) %collective-permute-start.17) | collective-permute-done | bytes 262176 | tf_op jit(solution)/shard_map/ppermute | solution.py:34
  74.6 4.5 %collective-permute-done.19.refs_6_ = bf16[64,2048]{1,0:T(8,128)(2,1)S(1)} collective-permute-done((bf16[64,2048]{1,0:T(8,128)(2,1)}, bf16[64,2048]{1,0:T(8,128)(2,1)S(1)}, u32[]{:S(2)}, u32[]{:S(2)}) %collective-permute-start.19) | collective-permute-done | bytes 262176 | tf_op jit(solution)/shard_map/ppermute | solution.py:34
  79.8 2.4 %collective-permute-start.20 = (bf16[32,2048]{1,0:T(8,128)(2,1)}, bf16[32,2048]{1,0:T(8,128)(2,1)S(1)}, u32[]{:S(2)}, u32[]{:S(2)}) collective-permute-start(bf16[32,2048]{1,0:T(8,128)(2,1)} %slice.30), channel_id=1, source_target_pairs={{0,28},{4,0},{8,4},{12,8},{16,12},{20,16},{24,20},{28,24},{1,29},{... | collective-permute-start | bytes 393224 | tf_op jit(solution)/shard_map/ppermute | solution.py:34
  82.8 2.1 %collective-permute-done.20.refs_5_ = bf16[32,2048]{1,0:T(8,128)(2,1)S(1)} collective-permute-done((bf16[32,2048]{1,0:T(8,128)(2,1)}, bf16[32,2048]{1,0:T(8,128)(2,1)S(1)}, u32[]{:S(2)}, u32[]{:S(2)}) %collective-permute-start.20) | collective-permute-done | bytes 131104 | tf_op jit(solution)/shard_map/ppermute | solution.py:34
  85.0 3.4 %collective-permute-done.16.refs_4_ = bf16[32,2048]{1,0:T(8,128)(2,1)} collective-permute-done((bf16[32,2048]{1,0:T(8,128)(2,1)}, bf16[32,2048]{1,0:T(8,128)(2,1)}, u32[]{:S(2)}, u32[]{:S(2)}) %collective-permute-start.16) | collective-permute-done | bytes 131104 | tf_op jit(solution)/shard_map/ppermute | solution.py:34
  90.3 11.0 %all_to_all.20.parts_ref = bf16[8,64,224]{2,1,0:T(8,128)(2,1)S(1)} all-to-all(bf16[8,64,224]{2,1,0:T(8,128)(2,1)S(1)} %bitcast.16), channel_id=1, replica_groups=mesh['head_0'=4,'head_1'=2,'expert_0'=8,'expert_1'=2,'expert_2'=2] {'hea..., dimensions={0} | all-to-all | bytes 458752 | tf_op jit(solution)/shard_map/all_to_all | solution.py:446
  102.4 9.8 %all-to-all-start.2 = ((bf16[32,24,224]{2,1,0:T(8,128)(2,1)}), bf16[32,24,224]{2,1,0:T(8,128)(2,1)S(1)}, u32[]{:S(2)}, u32[]{:S(2)}) async-start(bf16[32,24,224]{2,1,0:T(8,128)(2,1)} %copy-done.7), calls=%async_computation.2 | async-start | bytes 786432 | tf_op jit(solution)/shard_map/all_to_all | solution.py:446
  112.9 13.6 %all-to-all-done.2.x_ref = bf16[32,24,224]{2,1,0:T(8,128)(2,1)S(1)} async-done(((bf16[32,24,224]{2,1,0:T(8,128)(2,1)}), bf16[32,24,224]{2,1,0:T(8,128)(2,1)S(1)}, u32[]{:S(2)}, u32[]{:S(2)}) %all-to-all-start.2) | async-done | bytes 344096 | tf_op jit(solution)/shard_map/all_to_all | solution.py:446
  128.9 6.8 %collective-permute-done.23.refs_4_ = bf16[24,7168]{1,0:T(8,128)(2,1)S(1)} collective-permute-done((bf16[24,7168]{1,0:T(8,128)(2,1)S(1)}, bf16[24,7168]{1,0:T(8,128)(2,1)S(1)}, u32[]{:S(2)}, u32[]{:S(2)}) %collective-permute-start.23) | collective-permute-done | bytes 344096 | tf_op jit(solution)/shard_map/ppermute | solution.py:34
  138.4 2.8 %collective-permute-done.24.refs_3_ = bf16[24,3584]{1,0:T(8,128)(2,1)S(1)} collective-permute-done((bf16[24,3584]{1,0:T(8,128)(2,1)S(1)}, bf16[24,3584]{1,0:T(8,128)(2,1)S(1)}, u32[]{:S(2)}, u32[]{:S(2)}) %collective-permute-start.24) | collective-permute-done | bytes 172064 | tf_op jit(solution)/shard_map/ppermute | solution.py:34
  141.2 2.6 %collective-permute-done.22.refs_2_ = bf16[24,3584]{1,0:T(8,128)(2,1)S(1)} collective-permute-done((bf16[24,3584]{1,0:T(8,128)(2,1)S(1)}, bf16[24,3584]{1,0:T(8,128)(2,1)S(1)}, u32[]{:S(2)}, u32[]{:S(2)}) %collective-permute-start.22) | collective-permute-done | bytes 172064 | tf_op jit(solution)/shard_map/ppermute | solution.py:34
  150.4 2.3 %collective-permute-done.32.refs_3_ = bf16[192,128]{1,0:T(8,128)(2,1)S(1)} collective-permute-done((bf16[192,128]{1,0:T(8,128)(2,1)S(1)}, bf16[192,128]{1,0:T(8,128)(2,1)S(1)}, u32[]{:S(2)}, u32[]{:S(2)}) %collective-permute-start.32) | collective-permute-done | bytes 49184 | tf_op jit(solution)/shard_map/ppermute | solution.py:34
  161.7 3.0 %collective-permute-done.34.refs_1_ = bf16[24,1792]{1,0:T(8,128)(2,1)S(1)} collective-permute-done((bf16[24,1792]{1,0:T(8,128)(2,1)S(1)}, bf16[24,1792]{1,0:T(8,128)(2,1)S(1)}, u32[]{:S(2)}, u32[]{:S(2)}) %collective-permute-start.34) | collective-permute-done | bytes 86048 | tf_op jit(solution)/shard_map/ppermute | solution.py:34
  164.7 2.8 %collective-permute-done.35.refs_2_ = bf16[24,1792]{1,0:T(8,128)(2,1)S(1)} collective-permute-done((bf16[24,1792]{1,0:T(8,128)(2,1)S(1)}, bf16[24,1792]{1,0:T(8,128)(2,1)S(1)}, u32[]{:S(2)}, u32[]{:S(2)}) %collective-permute-start.35) | collective-permute-done | bytes 86048 | tf_op jit(solution)/shard_map/ppermute | solution.py:34
  169.1 20.3 %all_to_all.21.back_ref = bf16[32,24,224]{2,1,0:T(8,128)(2,1)S(1)} all-to-all(bf16[32,24,224]{2,1,0:T(8,128)(2,1)S(1)} %by_columns.1), channel_id=1, replica_groups=mesh['head_0'=4,'head_1'=2,'expert_0'=8,'expert_1'=2,'expert_2'=2] {'exp..., dimensions={0} | all-to-all | bytes 688128 | tf_op jit(solution)/shard_map/all_to_all | solution.py:446
  (126 shorter events, 62.5 us)
Async XLA Ops:
  3.3 31.2 %all-to-all-start = ((bf16[32,16,576]{2,1,0:T(8,128)(2,1)}), bf16[32,16,576]{2,1,0:T(8,128)(2,1)S(1)}, u32[]{:S(2)}, u32[]{:S(2)}) async-start(bf16[32,16,576]{2,1,0:T(8,128)(2,1)} %pack_cache.1), calls=%async_computation | async-start | bytes 1310720 | tf_op jit(solution)/shard_map/all_to_all | solution.py:446
  15.9 12.3 %collective-permute-start.1 = (bf16[128,1792]{1,0:T(8,128)(2,1)}, bf16[128,1792]{1,0:T(8,128)(2,1)}, u32[]{:S(2)}, u32[]{:S(2)}) collective-permute-start(bf16[128,1792]{1,0:T(8,128)(2,1)} %get-tuple-element.77), channel_id=1, source_target_pairs={{0,192},{64,0},{128,64},{192,128},{1,193},{65,1},{129,65},{193,129... | collective-permute-start | bytes 1376264 | tf_op jit(solution)/shard_map/ppermute | solution.py:34
  18.7 13.0 %collective-permute-start = (bf16[128,1792]{1,0:T(8,128)(2,1)}, bf16[128,1792]{1,0:T(8,128)(2,1)}, u32[]{:S(2)}, u32[]{:S(2)}) collective-permute-start(bf16[128,1792]{1,0:T(8,128)(2,1)} %get-tuple-element.79), channel_id=1, source_target_pairs={{0,64},{64,128},{128,192},{192,0},{1,65},{65,129},{129,193},{193,1... | collective-permute-start | bytes 1376264 | tf_op jit(solution)/shard_map/ppermute | solution.py:34
  38.6 6.7 %collective-permute-start.4 = (bf16[6,16,576]{2,1,0:T(8,128)(2,1)}, bf16[6,16,576]{2,1,0:T(8,128)(2,1)S(1)}, u32[]{:S(2)}, u32[]{:S(2)}) collective-permute-start(bf16[6,16,576]{2,1,0:T(8,128)(2,1)} %select_arrived.1.refs_0_), channel_id=1, source_target_pairs={{0,128},{64,192},{128,0},{192,64},{1,129},{65,193},{129,1},{193,65... | collective-permute-start | bytes 331784 | tf_op jit(solution)/shard_map/ppermute | solution.py:34
  39.4 7.1 %collective-permute-start.3 = (bf16[6,16,576]{2,1,0:T(8,128)(2,1)}, bf16[6,16,576]{2,1,0:T(8,128)(2,1)S(1)}, u32[]{:S(2)}, u32[]{:S(2)}) collective-permute-start(bf16[6,16,576]{2,1,0:T(8,128)(2,1)} %select_arrived.1.refs_0_), channel_id=1, source_target_pairs={{0,64},{64,128},{128,192},{192,0},{1,65},{65,129},{129,193},{193,1... | collective-permute-start | bytes 331784 | tf_op jit(solution)/shard_map/ppermute | solution.py:34
  40.3 6.3 %collective-permute-start.6 = (bf16[6,16,576]{2,1,0:T(8,128)(2,1)}, bf16[6,16,576]{2,1,0:T(8,128)(2,1)S(1)}, u32[]{:S(2)}, u32[]{:S(2)}) collective-permute-start(bf16[6,16,576]{2,1,0:T(8,128)(2,1)} %select_arrived.1.refs_0_), channel_id=1, source_target_pairs={{0,32},{32,0},{1,33},{33,1},{2,34},{34,2},{3,35},{35,3},{4,36},{36... | collective-permute-start | bytes 331784 | tf_op jit(solution)/shard_map/ppermute | solution.py:34
  52.9 6.1 %collective-permute-start.11 = (bf16[16,2048]{1,0:T(8,128)(2,1)S(1)}, bf16[16,2048]{1,0:T(8,128)(2,1)S(1)}, u32[]{:S(2)}, u32[]{:S(2)}) collective-permute-start(bf16[16,2048]{1,0:T(8,128)(2,1)S(1)} %new_attention.1.refs_0_), channel_id=1, source_target_pairs={{0,2},{1,3},{2,0},{3,1},{4,6},{5,7},{6,4},{7,5},{8,10},{9,11},{10,... | collective-permute-start | bytes 196616 | tf_op jit(solution)/shard_map/ppermute | solution.py:38
  59.0 6.7 %collective-permute-start.17 = (bf16[64,2048]{1,0:T(8,128)(2,1)S(1)}, bf16[64,2048]{1,0:T(8,128)(2,1)S(1)}, u32[]{:S(2)}, u32[]{:S(2)}) collective-permute-start(bf16[64,2048]{1,0:T(8,128)(2,1)S(1)} %stack.17.refs_0_), channel_id=1, source_target_pairs={{0,28},{4,0},{8,4},{12,8},{16,12},{20,16},{24,20},{28,24},{1,29},{... | collective-permute-start | bytes 786440 | tf_op jit(solution)/shard_map/ppermute | solution.py:34
  60.2 6.6 %collective-permute-start.13 = (bf16[64,2048]{1,0:T(8,128)(2,1)S(1)}, bf16[64,2048]{1,0:T(8,128)(2,1)S(1)}, u32[]{:S(2)}, u32[]{:S(2)}) collective-permute-start(bf16[64,2048]{1,0:T(8,128)(2,1)S(1)} %stack.17.refs_0_), channel_id=1, source_target_pairs={{0,4},{4,8},{8,12},{12,16},{16,20},{20,24},{24,28},{28,0},{1,5},{5... | collective-permute-start | bytes 786440 | tf_op jit(solution)/shard_map/ppermute | solution.py:34
  65.7 6.6 %collective-permute-start.18 = (bf16[64,2048]{1,0:T(8,128)(2,1)S(1)}, bf16[64,2048]{1,0:T(8,128)(2,1)}, u32[]{:S(2)}, u32[]{:S(2)}) collective-permute-start(bf16[64,2048]{1,0:T(8,128)(2,1)S(1)} %collective-permute-done.17.refs_8_), channel_id=1, source_target_pairs={{0,28},{4,0},{8,4},{12,8},{16,12},{20,16},{24,20},{28,24},{1,29},{... | collective-permute-start | bytes 786440 | tf_op jit(solution)/shard_map/ppermute | solution.py:34
  66.8 7.2 %collective-permute-start.14 = (bf16[64,2048]{1,0:T(8,128)(2,1)S(1)}, bf16[64,2048]{1,0:T(8,128)(2,1)}, u32[]{:S(2)}, u32[]{:S(2)}) collective-permute-start(bf16[64,2048]{1,0:T(8,128)(2,1)S(1)} %collective-permute-done.13.refs_1_), channel_id=1, source_target_pairs={{0,4},{4,8},{8,12},{12,16},{16,20},{20,24},{24,28},{28,0},{1,5},{5... | collective-permute-start | bytes 786440 | tf_op jit(solution)/shard_map/ppermute | solution.py:34
  69.4 13.4 %collective-permute-start.2 = (bf16[128,1792]{1,0:T(8,128)(2,1)}, bf16[128,1792]{1,0:T(8,128)(2,1)S(1)}, u32[]{:S(2)}, u32[]{:S(2)}) collective-permute-start(bf16[128,1792]{1,0:T(8,128)(2,1)} %get-tuple-element.44), channel_id=1, source_target_pairs={{0,128},{64,192},{128,0},{192,64},{1,129},{65,193},{129,1},{193,65... | collective-permute-start | bytes 1376264 | tf_op jit(solution)/shard_map/ppermute | solution.py:34
  72.3 6.8 %collective-permute-start.19 = (bf16[64,2048]{1,0:T(8,128)(2,1)}, bf16[64,2048]{1,0:T(8,128)(2,1)S(1)}, u32[]{:S(2)}, u32[]{:S(2)}) collective-permute-start(bf16[64,2048]{1,0:T(8,128)(2,1)} %collective-permute-done.18.refs_7_), channel_id=1, source_target_pairs={{0,28},{4,0},{8,4},{12,8},{16,12},{20,16},{24,20},{28,24},{1,29},{... | collective-permute-start | bytes 786440 | tf_op jit(solution)/shard_map/ppermute | solution.py:34
  74.0 8.1 %collective-permute-start.15 = (bf16[64,2048]{1,0:T(8,128)(2,1)}, bf16[64,2048]{1,0:T(8,128)(2,1)S(1)}, u32[]{:S(2)}, u32[]{:S(2)}) collective-permute-start(bf16[64,2048]{1,0:T(8,128)(2,1)} %collective-permute-done.14.refs_2_), channel_id=1, source_target_pairs={{0,4},{4,8},{8,12},{12,16},{16,20},{20,24},{24,28},{28,0},{1,5},{5... | collective-permute-start | bytes 786440 | tf_op jit(solution)/shard_map/ppermute | solution.py:34
  102.4 24.2 %all-to-all-start.2 = ((bf16[32,24,224]{2,1,0:T(8,128)(2,1)}), bf16[32,24,224]{2,1,0:T(8,128)(2,1)S(1)}, u32[]{:S(2)}, u32[]{:S(2)}) async-start(bf16[32,24,224]{2,1,0:T(8,128)(2,1)} %copy-done.7), calls=%async_computation.2 | async-start | bytes 786432 | tf_op jit(solution)/shard_map/all_to_all | solution.py:446
  126.7 8.9 %collective-permute-start.23 = (bf16[24,7168]{1,0:T(8,128)(2,1)S(1)}, bf16[24,7168]{1,0:T(8,128)(2,1)S(1)}, u32[]{:S(2)}, u32[]{:S(2)}) collective-permute-start(bf16[24,7168]{1,0:T(8,128)(2,1)S(1)} %norm.1.refs_0_), channel_id=1, source_target_pairs={{0,192},{64,0},{128,64},{192,128},{1,193},{65,1},{129,65},{193,129... | collective-permute-start | bytes 1032200 | tf_op jit(solution)/shard_map/ppermute | solution.py:34
  128.0 9.0 %collective-permute-start.21 = (bf16[24,7168]{1,0:T(8,128)(2,1)S(1)}, bf16[24,7168]{1,0:T(8,128)(2,1)S(1)}, u32[]{:S(2)}, u32[]{:S(2)}) collective-permute-start(bf16[24,7168]{1,0:T(8,128)(2,1)S(1)} %norm.1.refs_0_), channel_id=1, source_target_pairs={{0,64},{64,128},{128,192},{192,0},{1,65},{65,129},{129,193},{193,1... | collective-permute-start | bytes 1032200 | tf_op jit(solution)/shard_map/ppermute | solution.py:34
  128.8 14.9 %collective-permute-start.25 = (bf16[24,7168]{1,0:T(8,128)(2,1)S(1)}, bf16[24,7168]{1,0:T(8,128)(2,1)S(1)}, u32[]{:S(2)}, u32[]{:S(2)}) collective-permute-start(bf16[24,7168]{1,0:T(8,128)(2,1)S(1)} %norm.1.refs_0_), channel_id=1, source_target_pairs={{0,32},{32,0},{1,33},{33,1},{2,34},{34,2},{3,35},{35,3},{4,36},{36... | collective-permute-start | bytes 1032200 | tf_op jit(solution)/shard_map/ppermute | solution.py:34
  137.0 6.7 %collective-permute-start.22 = (bf16[24,3584]{1,0:T(8,128)(2,1)S(1)}, bf16[24,3584]{1,0:T(8,128)(2,1)S(1)}, u32[]{:S(2)}, u32[]{:S(2)}) collective-permute-start(bf16[24,3584]{1,0:T(8,128)(2,1)S(1)} %slice.31), channel_id=1, source_target_pairs={{0,64},{64,128},{128,192},{192,0},{1,65},{65,129},{129,193},{193,1... | collective-permute-start | bytes 516104 | tf_op jit(solution)/shard_map/ppermute | solution.py:34
  137.9 5.9 %collective-permute-start.29 = (bf16[24,7168]{1,0:T(8,128)(2,1)S(1)}, bf16[24,7168]{1,0:T(8,128)(2,1)S(1)}, u32[]{:S(2)}, u32[]{:S(2)}) collective-permute-start(bf16[24,7168]{1,0:T(8,128)(2,1)S(1)} %collective-permute-done.23.refs_4_), channel_id=1, source_target_pairs={{0,32},{32,0},{1,33},{33,1},{2,34},{34,2},{3,35},{35,3},{4,36},{36... | collective-permute-start | bytes 1032200 | tf_op jit(solution)/shard_map/ppermute | solution.py:34
  137.9 7.3 %collective-permute-start.26 = (bf16[24,7168]{1,0:T(8,128)(2,1)S(1)}, bf16[24,7168]{1,0:T(8,128)(2,1)S(1)}, u32[]{:S(2)}, u32[]{:S(2)}) collective-permute-start(bf16[24,7168]{1,0:T(8,128)(2,1)S(1)} %collective-permute-done.21.refs_1_), channel_id=1, source_target_pairs={{0,32},{32,0},{1,33},{33,1},{2,34},{34,2},{3,35},{35,3},{4,36},{36... | collective-permute-start | bytes 1032200 | tf_op jit(solution)/shard_map/ppermute | solution.py:34
  158.8 5.9 %collective-permute-start.34 = (bf16[24,1792]{1,0:T(8,128)(2,1)S(1)}, bf16[24,1792]{1,0:T(8,128)(2,1)S(1)}, u32[]{:S(2)}, u32[]{:S(2)}) collective-permute-start(bf16[24,1792]{1,0:T(8,128)(2,1)S(1)} %get-tuple-element.70), channel_id=1, source_target_pairs={{0,192},{64,0},{128,64},{192,128},{1,193},{65,1},{129,65},{193,129... | collective-permute-start | bytes 258056 | tf_op jit(solution)/shard_map/ppermute | solution.py:34
  160.7 6.7 %collective-permute-start.35 = (bf16[24,1792]{1,0:T(8,128)(2,1)S(1)}, bf16[24,1792]{1,0:T(8,128)(2,1)S(1)}, u32[]{:S(2)}, u32[]{:S(2)}) collective-permute-start(bf16[24,1792]{1,0:T(8,128)(2,1)S(1)} %get-tuple-element.71), channel_id=1, source_target_pairs={{0,128},{64,192},{128,0},{192,64},{1,129},{65,193},{129,1},{193,65... | collective-permute-start | bytes 258056 | tf_op jit(solution)/shard_map/ppermute | solution.py:34
  161.6 6.7 %collective-permute-start.36 = (bf16[24,1792]{1,0:T(8,128)(2,1)S(1)}, bf16[24,1792]{1,0:T(8,128)(2,1)S(1)}, u32[]{:S(2)}, u32[]{:S(2)}) collective-permute-start(bf16[24,1792]{1,0:T(8,128)(2,1)S(1)} %get-tuple-element.72), channel_id=1, source_target_pairs={{0,64},{64,128},{128,192},{192,0},{1,65},{65,129},{129,193},{193,1... | collective-permute-start | bytes 258056 | tf_op jit(solution)/shard_map/ppermute | solution.py:34
  (32 other events, 327.7 us)
